TPU v7x, 256 devices: a whole 4x4x8 slice. The times are simulated.
256 devices in a mesh: seq: 32 (over z, x), pipe: 2 (over core), dp: 4 (over y).
Axes of the slice: x: 4, y: 4, z: 8, core: 2. Of those that a mesh axis runs over, the one named last changes fastest.
Arguments:
- hidden_in: bfloat16 [4, 8192, 1536], P('dp', 'seq'), as said below
- upstream: bfloat16 [4, 8192, 1536], P('dp', 'seq'), as said below
- utt_lengths: int32 [4, 32], P('dp'), may hold values from 1 to 512, 8192 in all within a row
- weight: bfloat16 [2, 1536, 1536], P('pipe'), as said below
- kernel: float32 [2, 32, 1536], P('pipe'), may hold values from -1 to 1
- norm_gain: float32 [2, 1536], P('pipe'), may hold values from 0.1 to 1.9
- norm_bias: float32 [2, 1536], P('pipe'), may hold values from -3 to 3
Outputs:
- grad_input: bfloat16 [4, 8192, 1536], P('dp', 'seq', 'pipe')
- grad_weight: float32 [2, 1536, 1536], P('pipe', ('seq', 'dp'))
- grad_kernel: float32 [2, 32, 1536], P('pipe')
- grad_gain: float32 [2, 1536], P('pipe')
- grad_bias: float32 [2, 1536], P('pipe')
Inputs may be any that keep to these rules, and one draw needn't show every extreme that they name: `utt_lengths`: each bin's lengths sum to 8192; the longest utterance of every bin has exactly 512 frames. `hidden_in`: frame scales vary from frame to frame. `upstream`: entries of order one. `weight`: entries of order one over the square root of 1536.
All inputs are finite; a program needn't handle non-finite values.
Results may differ from a plain program's by a relative error of at most 0.019.
Values may be sent and summed in bfloat16 or wider, within the bound.
A program may use at most 128 MiB of HBM per device.

v0:
```python
import jax
import jax.numpy as jnp
from jax import lax
from jax.sharding import PartitionSpec as P

EPSILON = 1e-05
HIGHEST = lax.Precision.HIGHEST


def padded_2(block, sides, width):
    for axis, dim in sides:
        count = lax.axis_size(axis)
        forward = [(i, i + 1) for i in range(count - 1)]
        backward = [(target, source) for source, target in forward]
        low = lax.ppermute(
            lax.slice_in_dim(block, block.shape[dim] - width, None, axis=dim), axis, forward
        )
        high = lax.ppermute(lax.slice_in_dim(block, 0, width, axis=dim), axis, backward)
        block = jnp.concatenate([low, block, high], axis=dim)
    return block


def from_behind(x, axis, by):
    length = lax.axis_size(axis)
    pairs = [(i, i + by) for i in range(length) if 0 <= i + by < length]
    return lax.ppermute(x, axis, pairs)


def frame_ids(lengths, first_frame, frame_count):
    starts = jnp.cumsum(lengths) - lengths
    frames = first_frame + jnp.arange(frame_count, dtype=jnp.int32)
    owners = jnp.sum((starts[None, :] <= frames[:, None]).astype(jnp.int32), axis=1) - 1
    bin_total = jnp.sum(lengths)
    inside = (frames >= 0) & (frames < bin_total)
    return jnp.where(inside, owners, -2)


def depthwise(padded, padded_seg, kernel, frame_rows):
    tap_count = kernel.shape[0]
    centre = padded_seg[tap_count // 2 : tap_count // 2 + frame_rows]
    result = jnp.zeros((frame_rows, padded.shape[1]), jnp.float32)
    for tap_index in range(tap_count):
        window = padded[tap_index + 1 : tap_index + 1 + frame_rows].astype(jnp.float32)
        same_utt = (padded_seg[tap_index + 1 : tap_index + 1 + frame_rows] == centre)[:, None]
        result = result + jnp.where(same_utt, window * kernel[tap_index][None, :], 0.0)
    return result


def depthwise_back(padded_grad, padded_seg, kernel, frame_rows):
    tap_count = kernel.shape[0]
    centre = padded_seg[tap_count // 2 : tap_count // 2 + frame_rows]
    result = jnp.zeros((frame_rows, padded_grad.shape[1]), jnp.float32)
    for tap_index in range(tap_count):
        offset = tap_count - 1 - tap_index
        window = padded_grad[offset : offset + frame_rows].astype(jnp.float32)
        same_utt = (padded_seg[offset : offset + frame_rows] == centre)[:, None]
        result = result + jnp.where(same_utt, window * kernel[tap_index][None, :], 0.0)
    return result


def kernel_grad(padded, padded_seg, conv_grad, frame_rows, tap_count):
    centre = padded_seg[tap_count // 2 : tap_count // 2 + frame_rows]
    grad_float = conv_grad.astype(jnp.float32)
    pieces = []
    for tap_index in range(tap_count):
        window = padded[tap_index + 1 : tap_index + 1 + frame_rows].astype(jnp.float32)
        same_utt = (padded_seg[tap_index + 1 : tap_index + 1 + frame_rows] == centre)[:, None]
        pieces.append(jnp.sum(jnp.where(same_utt, window * grad_float, 0.0), axis=0))
    return jnp.stack(pieces)


def global_totals(partial_value):
    return lax.psum(partial_value, "seq")


def section_forward(hidden, lengths, kernel, gain, bias, weight, first_frame, totals_fn):
    frame_rows, model_width = hidden.shape
    rim_width = kernel.shape[0] // 2
    padded = padded_2(hidden, (("seq", 0),), rim_width)
    padded_seg = frame_ids(lengths, first_frame - rim_width, frame_rows + 2 * rim_width)
    frame_seg = padded_seg[rim_width : rim_width + frame_rows]
    conv_out = depthwise(padded, padded_seg, kernel, frame_rows)
    onehot = (frame_seg[:, None] == jnp.arange(lengths.shape[0], dtype=jnp.int32)[None, :]).astype(
        jnp.float32
    )
    stacked = jnp.stack([jnp.sum(conv_out, axis=1), jnp.sum(conv_out * conv_out, axis=1)])
    utt_table = totals_fn(jnp.dot(stacked, onehot, precision=HIGHEST))
    counts = lengths.astype(jnp.float32) * model_width
    means_utt = utt_table[0] / counts
    spread = utt_table[1] / counts - means_utt * means_utt
    inv_scale = lax.rsqrt(spread + EPSILON)
    frame_stats = jnp.dot(onehot, jnp.stack([means_utt, inv_scale], axis=1), precision=HIGHEST)
    normed = (conv_out - frame_stats[:, 0:1]) * frame_stats[:, 1:2]
    pre_act = normed * gain[None, :] + bias[None, :]
    activation = jax.nn.silu(pre_act).astype(jnp.bfloat16)
    product = jnp.dot(activation, weight, preferred_element_type=jnp.float32)
    output = (hidden.astype(jnp.float32) + product).astype(jnp.bfloat16)
    return (output, (padded, padded_seg, onehot, frame_stats, normed, pre_act, activation))


def section_backward(upstream_grad, saved_forward, lengths, kernel, gain, weight, totals_fn):
    padded, padded_seg, onehot, frame_stats, normed, pre_act, activation = saved_forward
    frame_rows, model_width = upstream_grad.shape
    act_grad = lax.dot_general(
        upstream_grad, weight, (((1,), (1,)), ((), ())), preferred_element_type=jnp.float32
    )
    sigmoid_out = jax.nn.sigmoid(pre_act)
    pre_grad = act_grad * sigmoid_out * (1.0 + pre_act * (1.0 - sigmoid_out))
    normed_grad = pre_grad * gain[None, :]
    stacked = jnp.stack([jnp.sum(normed_grad, axis=1), jnp.sum(normed_grad * normed, axis=1)])
    utt_table = totals_fn(jnp.dot(stacked, onehot, precision=HIGHEST))
    counts = lengths.astype(jnp.float32) * model_width
    per_frame = jnp.dot(onehot, (utt_table / counts[None, :]).T, precision=HIGHEST)
    conv_grad = (
        frame_stats[:, 1:2] * (normed_grad - per_frame[:, 0:1] - normed * per_frame[:, 1:2])
    ).astype(jnp.bfloat16)
    rim_width = kernel.shape[0] // 2
    padded_grad = padded_2(conv_grad, (("seq", 0),), rim_width)
    input_grad = (
        upstream_grad.astype(jnp.float32)
        + depthwise_back(padded_grad, padded_seg, kernel, frame_rows)
    ).astype(jnp.bfloat16)
    return (input_grad, conv_grad, pre_grad)


def body(hidden_in, upstream, utt_lengths, weight, kernel, norm_gain, norm_bias):
    hidden = hidden_in[0]
    cotangent = upstream[0]
    lengths = utt_lengths[0]
    section_weight = weight[0]
    section_kernel = kernel[0]
    section_gain = norm_gain[0]
    section_bias = norm_bias[0]
    frame_rows, model_width = hidden.shape
    first_frame = lax.axis_index("seq") * frame_rows
    section_id = lax.axis_index("pipe")
    sections = lax.axis_size("pipe")
    section_input = hidden
    section_output = hidden
    kept_forward = None
    for slot_index in range(sections):
        if slot_index > 0:
            section_input = from_behind(section_output, "pipe", 1)
        section_output, fresh_saved = section_forward(
            section_input,
            lengths,
            section_kernel,
            section_gain,
            section_bias,
            section_weight,
            first_frame,
            global_totals,
        )
        if kept_forward is None:
            kept_forward = fresh_saved
        else:
            kept_forward = jax.tree.map(
                lambda recent, earlier: jnp.where(section_id == slot_index, recent, earlier),
                fresh_saved,
                kept_forward,
            )
    upstream_grad = cotangent
    input_grad = cotangent
    own_backward = None
    for slot_index in range(sections - 1, -1, -1):
        if slot_index < sections - 1:
            upstream_grad = from_behind(input_grad, "pipe", -1)
        input_grad, conv_grad, pre_grad = section_backward(
            upstream_grad,
            kept_forward,
            lengths,
            section_kernel,
            section_gain,
            section_weight,
            global_totals,
        )
        fresh_backward = (upstream_grad, conv_grad, pre_grad)
        if own_backward is None:
            own_backward = fresh_backward
        else:
            own_backward = jax.tree.map(
                lambda recent, earlier: jnp.where(section_id == slot_index, recent, earlier),
                fresh_backward,
                own_backward,
            )
    own_upstream, own_conv_grad, own_pre_grad = own_backward
    padded, padded_seg, onehot, frame_stats, normed, pre_act, activation = kept_forward
    kernel_part = kernel_grad(
        padded, padded_seg, own_conv_grad, frame_rows, section_kernel.shape[0]
    )
    norm_parts = jnp.stack([jnp.sum(own_pre_grad * normed, axis=0), jnp.sum(own_pre_grad, axis=0)])
    kernel_sum, norm_sum = lax.psum((kernel_part, norm_parts), ("seq", "dp"))
    weight_rows = lax.psum_scatter(
        lax.dot_general(
            activation, own_upstream, (((0,), (0,)), ((), ())), preferred_element_type=jnp.float32
        ),
        ("seq", "dp"),
        scatter_dimension=0,
        tiled=True,
    )
    half_width = model_width // 2
    moved_half = from_behind(input_grad[:, half_width:], "pipe", 1)
    grad_half = jnp.where(section_id == 0, input_grad[:, :half_width], moved_half)
    return (
        grad_half[None],
        weight_rows[None],
        kernel_sum[None],
        norm_sum[0][None],
        norm_sum[1][None],
    )


def solution(mesh):
    return jax.shard_map(
        body,
        mesh=mesh,
        in_specs=(
            P("dp", "seq", None),
            P("dp", "seq", None),
            P("dp", None),
            P("pipe", None, None),
            P("pipe", None, None),
            P("pipe", None),
            P("pipe", None),
        ),
        out_specs=(
            P("dp", "seq", "pipe"),
            P("pipe", ("seq", "dp"), None),
            P("pipe", None, None),
            P("pipe", None),
            P("pipe", None),
        ),
        check_vma=False,
    )
```

profile of v0, /device:TPU:1, one launch (start us, length us, event | category | flops | bytes accessed | tf_op | source)
XLA Modules:
  0.0 1940.2 jit_solution(18055696463895430105)
XLA Ops:
  8.0 3.9 collective-permute-start
  17.4 1.9 slice_reduce_fusion.31
  19.3 1.6 slice_reduce_fusion.30
  22.3 1.3 reduce.34
  23.6 28.1 %fusion.260 = (f32[256]{0:T(256)S(1)}, f32[256]{0:T(256)S(1)}, f32[256,1536]{1,0:T(8,128)S(1)}) fusion(f32[1536]{0:T(1024)S(1)} %get-tuple-element.92, bf16[16,1536]{1,0:T(8,128)(2,1)S(1)} %collective-permute-done.1, bf16[256,1536]{1,0:T(8,128)(2,1)} %bitcast.85, pred[256]{0:T(512)(128)(4,1)} %get-tuple-element.118, f32[1536]{0:T(1024)S(1)} %get-tuple-element.93, ...), kind=kLoop, calls=%fused_computation.533 | loop fusion | flops 87293440 | bytes 2664192 | tf_op jit(solution)/shard_map/reduce_sum | solution.py:86
  53.0 64.8 %psum.42 = f32[2,32]{1,0:T(2,128)S(1)} all-reduce(f32[2,32]{1,0:T(2,128)S(1)} %fusion.214), channel_id=1, replica_groups=mesh['seq'=32,'pipe'=2,'dp'=4] {'seq'}, use_global_device_ids=true, to_apply=%region_5.6 | all-reduce | flops 64 | bytes 512 | tf_op jit(solution)/shard_map/psum | solution.py:73
  118.8 3.9 fusion.22
  124.0 16.7 collective-permute-done.2
  143.3 1.8 collective-permute-start.4
  145.3 3.1 collective-permute-done.4
  149.0 12.2 fusion.259
  162.1 55.9 %psum.43 = f32[2,32]{1,0:T(2,128)S(1)} all-reduce(f32[2,32]{1,0:T(2,128)S(1)} %fusion.212), channel_id=1, replica_groups=mesh['seq'=32,'pipe'=2,'dp'=4] {'seq'}, use_global_device_ids=true, to_apply=%region_8.9 | all-reduce | flops 64 | bytes 512 | tf_op jit(solution)/shard_map/psum | solution.py:73
  220.3 7.3 multiply_reduce_fusion.6
  228.5 57.5 %psum.44 = f32[2,32]{1,0:T(2,128)S(1)} all-reduce(f32[2,32]{1,0:T(2,128)S(1)} %fusion.209), channel_id=1, replica_groups=mesh['seq'=32,'pipe'=2,'dp'=4] {'seq'}, use_global_device_ids=true, to_apply=%region_11.12 | all-reduce | flops 64 | bytes 512 | tf_op jit(solution)/shard_map/psum | solution.py:73
  287.2 2.3 multiply_convert_fusion.2
  289.5 1.9 collective-permute-start.6
  292.7 3.8 collective-permute-done.5
  296.9 19.7 %add_convert_fusion.1 = bf16[256,1536]{1,0:T(8,128)(2,1)} fusion(bf16[256,1536]{1,0:T(8,128)(2,1)S(1)} %multiply_convert_fusion.2, bf16[16,1536]{1,0:T(8,128)(2,1)S(1)} %collective-permute-done.5, bf16[16,1536]{1,0:T(8,128)(2,1)S(1)} %collective-permute-done.6, bf16[1,256,1536]{2,1,0:T(8,128)(2,1)S(1)} %copy-done.4, f32[1536]{0:T(1024)S(1)} %get-tuple-element.92, ...), kind=kLoop, calls=%fused_computation.217 | loop fusion | flops 87293952 | bytes 2662144 | tf_op jit(solution)/shard_map/convert_element_type | solution.py:122
  316.6 33.3 %collective-permute-start.7 = (bf16[256,1536]{1,0:T(8,128)(2,1)}, bf16[256,1536]{1,0:T(8,128)(2,1)}, u32[]{:S(2)}, u32[]{:S(2)}) collective-permute-start(bf16[256,1536]{1,0:T(8,128)(2,1)} %add_convert_fusion.1), channel_id=1, source_target_pairs={{4,0},{5,1},{6,2},{7,3},{12,8},{13,9},{14,10},{15,11},{20,16},{21,... | collective-permute-start | bytes 2359304 | tf_op jit(solution)/shard_map/ppermute | solution.py:26
  351.4 7.5 fusion.108
  359.0 381.5 %fusion = f32[16,1536]{1,0:T(8,128)S(1)} fusion(f32[1536,1536]{1,0:T(8,128)} %fusion.108), kind=kCustom, calls=%all-reduce-scatter | all-reduce-scatter fusion | flops 3145729 | bytes 9536512
  741.2 2.0 collective-permute-start.41
  743.2 1.9 collective-permute-start.40
  745.2 8.4 multiply_reduce_fusion
  754.5 63.6 %psum.45 = f32[2,32]{1,0:T(2,128)S(1)} all-reduce(f32[2,32]{1,0:T(2,128)S(1)} %fusion.207), channel_id=1, replica_groups=mesh['seq'=32,'pipe'=2,'dp'=4] {'seq'}, use_global_device_ids=true, to_apply=%region_14.15 | all-reduce | flops 64 | bytes 512 | tf_op jit(solution)/shard_map/psum | solution.py:73
  819.0 2.2 collective-permute-start.42
  821.2 6.7 fusion.100
  827.9 1.9 collective-permute-start.9
  832.3 1.9 collective-permute-start.39
  834.7 5.2 collective-permute-start.38
  839.9 3.5 collective-permute-start.37
  843.5 5.3 collective-permute-start.36
  848.8 2.7 collective-permute-start.35
  851.6 5.6 fusion.102
  857.2 1.3 collective-permute-start.34
  858.5 8.3 collective-permute-start.33
  866.8 2.2 collective-permute-start.32
  869.1 1.3 collective-permute-start.31
  870.4 1.3 collective-permute-start.30
  871.8 5.0 fusion.104
  876.9 2.1 collective-permute-start.29
  879.0 2.1 collective-permute-start.28
  881.2 2.9 collective-permute-start.27
  884.1 1.9 collective-permute-start.26
  886.0 5.5 collective-permute-start.25
  891.6 2.7 fusion.98
  894.4 1.3 collective-permute-start.24
  895.7 2.2 collective-permute-start.23
  898.0 1.3 collective-permute-start.22
  899.3 4.0 collective-permute-start.21
  904.0 2.8 collective-permute-start.20
  906.8 571.3 %psum.47 = f32[2,1536]{1,0:T(2,128)S(1)} all-reduce(f32[2,1536]{1,0:T(2,128)S(1)} %pad_maximum_fusion.6), channel_id=1, replica_groups=mesh['seq'=32,'pipe'=2,'dp'=4] {'seq','dp'}, use_global_device_ids=true, to_apply=%region_51.52 | all-reduce | flops 3072 | bytes 24576 | tf_op jit(solution)/shard_map/psum | solution.py:192
  1478.4 1.4 collective-permute-start.19
  1479.9 1.3 collective-permute-start.18
  1481.2 1.3 collective-permute-start.17
  1482.5 1.3 collective-permute-start.16
  1485.2 23.8 %add_convert_fusion = bf16[256,1536]{1,0:T(8,128)(2,1)S(1)} fusion(bf16[256,1536]{1,0:T(8,128)(2,1)S(1)} %get-tuple-element.95, bf16[256,1536]{1,0:T(8,128)(2,1)} %collective-permute-done.7, bf16[16,1536]{1,0:T(8,128)(2,1)} %collective-permute-done.8, bf16[16,1536]{1,0:T(8,128)(2,1)} %collective-permute-done.9, f32[1536]{0:T(1024)S(1)} %copy-done.14, ...), kind=kLoop, calls=%fused_computation.214 | loop fusion | flops 87293952 | bytes 2662144 | tf_op jit(solution)/shard_map/convert_element_type | solution.py:122
  1514.7 200.1 %collective-permute-start.11 = (f32[16,1536]{1,0:T(8,128)S(1)}, f32[16,1536]{1,0:T(8,128)}, u32[]{:S(2)}, u32[]{:S(2)}) collective-permute-start(f32[16,1536]{1,0:T(8,128)S(1)} %fusion), channel_id=1, source_target_pairs={{0,1},{1,2},{2,3},{3,8},{8,9},{9,10},{10,11},{11,16},{16,17},{17,1... | collective-permute-start | bytes 294920
  1714.8 1.5 collective-permute-start.10
  1717.7 2.8 stack.200
  1721.9 30.1 %concatenate.158 = f32[524,1536]{1,0:T(8,128)S(1)} concatenate(f32[12,1536]{1,0:T(8,128)} %collective-permute-done.42, f32[16,1536]{1,0:T(8,128)} %collective-permute-done.41, f32[16,1536]{1,0:T(8,128)} %collective-permute-done.40, f32[16,1536]{1,0:T(8,128)S(1)} %copy-done.23, f32[16,1536]{1,0:T(8,128)S(1)} %copy-done.25, f32[16,1536]{1,0:T(8,128)} %copy-done.26, ...), dimensions={0} | concatenate | bytes 6438912
  1752.7 1.9 fusion.206
  1754.6 176.9 %all-reduce.4.cloned.1.call-done = f32[1,32,1536]{2,1,0:T(8,128)} async-done(((f32[1,32,1536]{2,1,0:T(8,128)}), f32[1,32,1536]{2,1,0:T(8,128)}) %all-reduce.4.cloned.1.call-update) | async-done | bytes 196624 | tf_op jit(solution)/shard_map/psum | solution.py:192
  1931.5 1.6 copy.18
  (486 shorter events, 37.4 us)
Async XLA Ops:
  7.2 1924.4 %all-reduce.4.cloned.1.call-start = ((), (), s32[]{:S(2)}) async-start(), calls=%async_computation | async-start | bytes 393216 | tf_op jit(solution)/shard_map/psum | solution.py:192
  8.0 15.6 collective-permute-start
  12.0 11.6 collective-permute-start.1
  20.9 275.7 %copy-start.5 = (f32[1536]{0:T(1024)}, f32[1536]{0:T(1024)S(1)}, u32[]{:S(2)}) copy-start(f32[1536]{0:T(1024)S(1)} %get-tuple-element.88) | copy-start | bytes 18436
  20.9 275.7 %copy-start.7 = (f32[1536]{0:T(1024)}, f32[1536]{0:T(1024)S(1)}, u32[]{:S(2)}) copy-start(f32[1536]{0:T(1024)S(1)} %get-tuple-element.89) | copy-start | bytes 18436
  20.9 275.7 %copy-start.9 = (f32[1536]{0:T(1024)}, f32[1536]{0:T(1024)S(1)}, u32[]{:S(2)}) copy-start(f32[1536]{0:T(1024)S(1)} %get-tuple-element.90) | copy-start | bytes 18436
  20.9 275.7 %copy-start.11 = (f32[1536]{0:T(1024)}, f32[1536]{0:T(1024)S(1)}, u32[]{:S(2)}) copy-start(f32[1536]{0:T(1024)S(1)} %get-tuple-element.91) | copy-start | bytes 18436
  20.9 275.7 %copy-start.13 = (f32[1536]{0:T(1024)}, f32[1536]{0:T(1024)S(1)}, u32[]{:S(2)}) copy-start(f32[1536]{0:T(1024)S(1)} %get-tuple-element.92) | copy-start | bytes 18436
  122.7 18.0 collective-permute-start.2
  141.4 3.7 collective-permute-start.3
  143.3 5.0 collective-permute-start.4
  289.5 3.2 collective-permute-start.6
  291.4 5.1 collective-permute-start.5
  316.6 34.7 %collective-permute-start.7 = (bf16[256,1536]{1,0:T(8,128)(2,1)}, bf16[256,1536]{1,0:T(8,128)(2,1)}, u32[]{:S(2)}, u32[]{:S(2)}) collective-permute-start(bf16[256,1536]{1,0:T(8,128)(2,1)} %add_convert_fusion.1), channel_id=1, source_target_pairs={{4,0},{5,1},{6,2},{7,3},{12,8},{13,9},{14,10},{15,11},{20,16},{21,... | collective-permute-start | bytes 2359304 | tf_op jit(solution)/shard_map/ppermute | solution.py:26
  359.0 386.2 %copy-start.55 = (f32[1536]{0:T(1024)S(1)}, f32[1536]{0:T(1024)}, u32[]{:S(2)}) copy-start(f32[1536]{0:T(1024)} %copy-done.52) | copy-start | bytes 18436
  359.0 386.2 %copy-start.167 = (f32[256,1]{0,1:T(1,128)S(1)}, f32[256,1]{0,1:T(1,128)}, u32[]{:S(2)}) copy-start(f32[256,1]{0,1:T(1,128)} %copy-done.165) | copy-start | bytes 3076
  359.0 386.2 %copy-start.170 = (f32[256,1]{0,1:T(1,128)S(1)}, f32[256,1]{0,1:T(1,128)}, u32[]{:S(2)}) copy-start(f32[256,1]{0,1:T(1,128)} %copy-done.168) | copy-start | bytes 3076
  359.0 386.2 %copy-start.173 = (f32[256,1]{0,1:T(1,128)S(1)}, f32[256,1]{0,1:T(1,128)}, u32[]{:S(2)}) copy-start(f32[256,1]{0,1:T(1,128)} %copy-done.171) | copy-start | bytes 3076
  359.0 386.2 %copy-start.176 = (f32[256,1]{0,1:T(1,128)S(1)}, f32[256,1]{0,1:T(1,128)}, u32[]{:S(2)}) copy-start(f32[256,1]{0,1:T(1,128)} %copy-done.174) | copy-start | bytes 3076
  741.2 102.3 %collective-permute-start.41 = (f32[16,1536]{1,0:T(8,128)S(1)}, f32[16,1536]{1,0:T(8,128)}, u32[]{:S(2)}, u32[]{:S(2)}) collective-permute-start(f32[16,1536]{1,0:T(8,128)S(1)} %fusion), channel_id=1, source_target_pairs={{0,59},{1,64},{2,65},{3,66},{8,67},{9,72},{10,73},{11,74},{16,75},... | collective-permute-start | bytes 294920
  743.2 105.6 %collective-permute-start.40 = (f32[16,1536]{1,0:T(8,128)S(1)}, f32[16,1536]{1,0:T(8,128)}, u32[]{:S(2)}, u32[]{:S(2)}) collective-permute-start(f32[16,1536]{1,0:T(8,128)S(1)} %fusion), channel_id=1, source_target_pairs={{0,58},{1,59},{2,64},{3,65},{8,66},{9,67},{10,72},{11,73},{16,74},... | collective-permute-start | bytes 294920
  819.0 20.9 %collective-permute-start.42 = (f32[12,1536]{1,0:T(8,128)}, f32[12,1536]{1,0:T(8,128)}, u32[]{:S(2)}, u32[]{:S(2)}) collective-permute-start(f32[12,1536]{1,0:T(8,128)} %slice.1636), channel_id=1, source_target_pairs={{0,64},{1,65},{2,66},{3,67},{8,72},{9,73},{10,74},{11,75},{16,80},... | collective-permute-start | bytes 221192
  827.9 4.4 collective-permute-start.9
  829.8 4.9 collective-permute-start.8
  832.3 24.8 %collective-permute-start.39 = (f32[16,1536]{1,0:T(8,128)S(1)}, f32[16,1536]{1,0:T(8,128)S(1)}, u32[]{:S(2)}, u32[]{:S(2)}) collective-permute-start(f32[16,1536]{1,0:T(8,128)S(1)} %fusion), channel_id=1, source_target_pairs={{0,57},{1,58},{2,59},{3,64},{8,65},{9,66},{10,67},{11,72},{16,73},... | collective-permute-start | bytes 294920
  834.7 23.8 %collective-permute-start.38 = (f32[16,1536]{1,0:T(8,128)S(1)}, f32[16,1536]{1,0:T(8,128)S(1)}, u32[]{:S(2)}, u32[]{:S(2)}) collective-permute-start(f32[16,1536]{1,0:T(8,128)S(1)} %fusion), channel_id=1, source_target_pairs={{0,56},{1,57},{2,58},{3,59},{8,64},{9,65},{10,66},{11,67},{16,72},... | collective-permute-start | bytes 294920
  839.9 26.9 %collective-permute-start.37 = (f32[16,1536]{1,0:T(8,128)S(1)}, f32[16,1536]{1,0:T(8,128)S(1)}, u32[]{:S(2)}, u32[]{:S(2)}) collective-permute-start(f32[16,1536]{1,0:T(8,128)S(1)} %fusion), channel_id=1, source_target_pairs={{0,51},{1,56},{2,57},{3,58},{8,59},{9,64},{10,65},{11,66},{16,67},... | collective-permute-start | bytes 294920
  843.5 25.6 %collective-permute-start.36 = (f32[16,1536]{1,0:T(8,128)S(1)}, f32[16,1536]{1,0:T(8,128)S(1)}, u32[]{:S(2)}, u32[]{:S(2)}) collective-permute-start(f32[16,1536]{1,0:T(8,128)S(1)} %fusion), channel_id=1, source_target_pairs={{0,50},{1,51},{2,56},{3,57},{8,58},{9,59},{10,64},{11,65},{16,66},... | collective-permute-start | bytes 294920
  848.8 21.5 %collective-permute-start.35 = (f32[16,1536]{1,0:T(8,128)S(1)}, f32[16,1536]{1,0:T(8,128)S(1)}, u32[]{:S(2)}, u32[]{:S(2)}) collective-permute-start(f32[16,1536]{1,0:T(8,128)S(1)} %fusion), channel_id=1, source_target_pairs={{0,49},{1,50},{2,51},{3,56},{8,57},{9,58},{10,59},{11,64},{16,65},... | collective-permute-start | bytes 294920
  857.2 19.7 %collective-permute-start.34 = (f32[16,1536]{1,0:T(8,128)S(1)}, f32[16,1536]{1,0:T(8,128)S(1)}, u32[]{:S(2)}, u32[]{:S(2)}) collective-permute-start(f32[16,1536]{1,0:T(8,128)S(1)} %fusion), channel_id=1, source_target_pairs={{0,48},{1,49},{2,50},{3,51},{8,56},{9,57},{10,58},{11,59},{16,64},... | collective-permute-start | bytes 294920
  858.5 20.5 %collective-permute-start.33 = (f32[16,1536]{1,0:T(8,128)S(1)}, f32[16,1536]{1,0:T(8,128)S(1)}, u32[]{:S(2)}, u32[]{:S(2)}) collective-permute-start(f32[16,1536]{1,0:T(8,128)S(1)} %fusion), channel_id=1, source_target_pairs={{0,43},{1,48},{2,49},{3,50},{8,51},{9,56},{10,57},{11,58},{16,59},... | collective-permute-start | bytes 294920
  866.8 14.3 collective-permute-start.32
  869.1 15.0 collective-permute-start.31
  870.4 15.6 collective-permute-start.30
  876.8 608.3 %copy-start.6 = (f32[1536]{0:T(1024)S(1)}, f32[1536]{0:T(1024)}, u32[]{:S(2)}) copy-start(f32[1536]{0:T(1024)} %copy-done.5) | copy-start | bytes 18436
  876.8 608.3 %copy-start.8 = (f32[1536]{0:T(1024)S(1)}, f32[1536]{0:T(1024)}, u32[]{:S(2)}) copy-start(f32[1536]{0:T(1024)} %copy-done.7) | copy-start | bytes 18436
  876.8 608.3 %copy-start.10 = (f32[1536]{0:T(1024)S(1)}, f32[1536]{0:T(1024)}, u32[]{:S(2)}) copy-start(f32[1536]{0:T(1024)} %copy-done.9) | copy-start | bytes 18436
  876.8 608.3 %copy-start.12 = (f32[1536]{0:T(1024)S(1)}, f32[1536]{0:T(1024)}, u32[]{:S(2)}) copy-start(f32[1536]{0:T(1024)} %copy-done.11) | copy-start | bytes 18436
  876.9 608.3 %copy-start.14 = (f32[1536]{0:T(1024)S(1)}, f32[1536]{0:T(1024)}, u32[]{:S(2)}) copy-start(f32[1536]{0:T(1024)} %copy-done.13) | copy-start | bytes 18436
  876.9 608.3 %copy-start.16 = (f32[1536]{0:T(1024)S(1)}, f32[1536]{0:T(1024)}, u32[]{:S(2)}) copy-start(f32[1536]{0:T(1024)} %copy-done.15) | copy-start | bytes 18436
  876.9 17.5 collective-permute-start.29
  879.0 16.7 collective-permute-start.28
  881.2 16.8 collective-permute-start.27
  884.1 15.2 collective-permute-start.26
  886.0 17.3 collective-permute-start.25
  894.4 616.3 %copy-start.34 = (f32[16,1536]{1,0:T(8,128)}, f32[16,1536]{1,0:T(8,128)S(1)}, u32[]{:S(2)}) copy-start(f32[16,1536]{1,0:T(8,128)S(1)} %collective-permute-done.29) | copy-start | bytes 294916
  894.4 584.0 %collective-permute-start.24 = (f32[16,1536]{1,0:T(8,128)S(1)}, f32[16,1536]{1,0:T(8,128)S(1)}, u32[]{:S(2)}, u32[]{:S(2)}) collective-permute-start(f32[16,1536]{1,0:T(8,128)S(1)} %fusion), channel_id=1, source_target_pairs={{0,26},{1,27},{2,32},{3,33},{8,34},{9,35},{10,40},{11,41},{16,42},... | collective-permute-start | bytes 294920
  895.7 614.9 %copy-start.35 = (f32[16,1536]{1,0:T(8,128)}, f32[16,1536]{1,0:T(8,128)S(1)}, u32[]{:S(2)}) copy-start(f32[16,1536]{1,0:T(8,128)S(1)} %collective-permute-done.28) | copy-start | bytes 294916
  895.7 584.1 %collective-permute-start.23 = (f32[16,1536]{1,0:T(8,128)S(1)}, f32[16,1536]{1,0:T(8,128)S(1)}, u32[]{:S(2)}, u32[]{:S(2)}) collective-permute-start(f32[16,1536]{1,0:T(8,128)S(1)} %fusion), channel_id=1, source_target_pairs={{0,25},{1,26},{2,27},{3,32},{8,33},{9,34},{10,35},{11,40},{16,41},... | collective-permute-start | bytes 294920
  898.0 612.7 %copy-start.36 = (f32[16,1536]{1,0:T(8,128)}, f32[16,1536]{1,0:T(8,128)S(1)}, u32[]{:S(2)}) copy-start(f32[16,1536]{1,0:T(8,128)S(1)} %collective-permute-done.27) | copy-start | bytes 294916
  898.0 583.2 %collective-permute-start.22 = (f32[16,1536]{1,0:T(8,128)S(1)}, f32[16,1536]{1,0:T(8,128)S(1)}, u32[]{:S(2)}, u32[]{:S(2)}) collective-permute-start(f32[16,1536]{1,0:T(8,128)S(1)} %fusion), channel_id=1, source_target_pairs={{0,24},{1,25},{2,26},{3,27},{8,32},{9,33},{10,34},{11,35},{16,40},... | collective-permute-start | bytes 294920
  899.3 611.4 %copy-start.37 = (f32[16,1536]{1,0:T(8,128)}, f32[16,1536]{1,0:T(8,128)S(1)}, u32[]{:S(2)}) copy-start(f32[16,1536]{1,0:T(8,128)S(1)} %collective-permute-done.26) | copy-start | bytes 294916
  899.3 583.2 %collective-permute-start.21 = (f32[16,1536]{1,0:T(8,128)S(1)}, f32[16,1536]{1,0:T(8,128)S(1)}, u32[]{:S(2)}, u32[]{:S(2)}) collective-permute-start(f32[16,1536]{1,0:T(8,128)S(1)} %fusion), channel_id=1, source_target_pairs={{0,19},{1,24},{2,25},{3,26},{8,27},{9,32},{10,33},{11,34},{16,35},... | collective-permute-start | bytes 294920
  904.0 579.8 %collective-permute-start.20 = (f32[16,1536]{1,0:T(8,128)S(1)}, f32[16,1536]{1,0:T(8,128)S(1)}, u32[]{:S(2)}, u32[]{:S(2)}) collective-permute-start(f32[16,1536]{1,0:T(8,128)S(1)} %fusion), channel_id=1, source_target_pairs={{0,18},{1,19},{2,24},{3,25},{8,26},{9,27},{10,32},{11,33},{16,34},... | collective-permute-start | bytes 294920
  1478.4 32.3 %collective-permute-start.19 = (f32[16,1536]{1,0:T(8,128)S(1)}, f32[16,1536]{1,0:T(8,128)S(1)}, u32[]{:S(2)}, u32[]{:S(2)}) collective-permute-start(f32[16,1536]{1,0:T(8,128)S(1)} %fusion), channel_id=1, source_target_pairs={{0,17},{1,18},{2,19},{3,24},{8,25},{9,26},{10,27},{11,32},{16,33},... | collective-permute-start | bytes 294920
  1479.9 32.2 %collective-permute-start.18 = (f32[16,1536]{1,0:T(8,128)S(1)}, f32[16,1536]{1,0:T(8,128)S(1)}, u32[]{:S(2)}, u32[]{:S(2)}) collective-permute-start(f32[16,1536]{1,0:T(8,128)S(1)} %fusion), channel_id=1, source_target_pairs={{0,16},{1,17},{2,18},{3,19},{8,24},{9,25},{10,26},{11,27},{16,32},... | collective-permute-start | bytes 294920
  1481.2 32.2 %collective-permute-start.17 = (f32[16,1536]{1,0:T(8,128)S(1)}, f32[16,1536]{1,0:T(8,128)S(1)}, u32[]{:S(2)}, u32[]{:S(2)}) collective-permute-start(f32[16,1536]{1,0:T(8,128)S(1)} %fusion), channel_id=1, source_target_pairs={{0,11},{1,16},{2,17},{3,18},{8,19},{9,24},{10,25},{11,26},{16,27},... | collective-permute-start | bytes 294920
  1482.5 32.2 %collective-permute-start.16 = (f32[16,1536]{1,0:T(8,128)S(1)}, f32[16,1536]{1,0:T(8,128)S(1)}, u32[]{:S(2)}, u32[]{:S(2)}) collective-permute-start(f32[16,1536]{1,0:T(8,128)S(1)} %fusion), channel_id=1, source_target_pairs={{0,10},{1,11},{2,16},{3,17},{8,18},{9,19},{10,24},{11,25},{16,26},... | collective-permute-start | bytes 294920
  1483.8 231.0 %collective-permute-start.15 = (f32[16,1536]{1,0:T(8,128)S(1)}, f32[16,1536]{1,0:T(8,128)S(1)}, u32[]{:S(2)}, u32[]{:S(2)}) collective-permute-start(f32[16,1536]{1,0:T(8,128)S(1)} %fusion), channel_id=1, source_target_pairs={{0,9},{1,10},{2,11},{3,16},{8,17},{9,18},{10,19},{11,24},{16,25},{... | collective-permute-start | bytes 294920
  1510.7 209.8 %collective-permute-start.14 = (f32[16,1536]{1,0:T(8,128)S(1)}, f32[16,1536]{1,0:T(8,128)S(1)}, u32[]{:S(2)}, u32[]{:S(2)}) collective-permute-start(f32[16,1536]{1,0:T(8,128)S(1)} %fusion), channel_id=1, source_target_pairs={{0,8},{1,9},{2,10},{3,11},{8,16},{9,17},{10,18},{11,19},{16,24},{1... | collective-permute-start | bytes 294920
  1512.1 208.5 %collective-permute-start.13 = (f32[16,1536]{1,0:T(8,128)S(1)}, f32[16,1536]{1,0:T(8,128)S(1)}, u32[]{:S(2)}, u32[]{:S(2)}) collective-permute-start(f32[16,1536]{1,0:T(8,128)S(1)} %fusion), channel_id=1, source_target_pairs={{0,3},{1,8},{2,9},{3,10},{8,11},{9,16},{10,17},{11,18},{16,19},{17... | collective-permute-start | bytes 294920
  1513.4 207.2 %collective-permute-start.12 = (f32[16,1536]{1,0:T(8,128)S(1)}, f32[16,1536]{1,0:T(8,128)S(1)}, u32[]{:S(2)}, u32[]{:S(2)}) collective-permute-start(f32[16,1536]{1,0:T(8,128)S(1)} %fusion), channel_id=1, source_target_pairs={{0,2},{1,3},{2,8},{3,9},{8,10},{9,11},{10,16},{11,17},{16,18},{17,... | collective-permute-start | bytes 294920
  1514.7 207.1 %collective-permute-start.11 = (f32[16,1536]{1,0:T(8,128)S(1)}, f32[16,1536]{1,0:T(8,128)}, u32[]{:S(2)}, u32[]{:S(2)}) collective-permute-start(f32[16,1536]{1,0:T(8,128)S(1)} %fusion), channel_id=1, source_target_pairs={{0,1},{1,2},{2,3},{3,8},{8,9},{9,10},{10,11},{11,16},{16,17},{17,1... | collective-permute-start | bytes 294920
  1714.8 37.8 %collective-permute-start.10 = (bf16[256,768]{1,0:T(8,128)(2,1)}, bf16[256,768]{1,0:T(8,128)(2,1)}, u32[]{:S(2)}, u32[]{:S(2)}) collective-permute-start(bf16[256,768]{1,0:T(8,128)(2,1)} %slice.1601), channel_id=1, source_target_pairs={{0,4},{1,5},{2,6},{3,7},{8,12},{9,13},{10,14},{11,15},{16,20},{17,... | collective-permute-start | bytes 1179656 | tf_op jit(solution)/shard_map/ppermute | solution.py:26
  (160 other events, 12273.3 us)
Sparse Core Ops, SparseCore 0:
  1720.7 210.8 all-reduce.3
where the time goes:
time: 1950 us; the launch traced here: 1940 us
  blocking collectives  1190 us (61%)
  starting transfers between devices  327 us (17%)
  waiting for transfers between devices  201 us (10%)
  other arithmetic  117 us (6%)
  local copies, waits for them, and re-layouts  48.1 us (2%)
  matrix products  34.3 us (2%)
    psum x1, blocking collectives, body(): kernel_sum, norm_sum = lax.psum((kernel_part, norm_parts), ('seq', 'dp'))  571 us
    unnamed x1, blocking collectives  382 us
    unnamed x32, starting transfers between devices  276 us
    psum x4, blocking collectives, global_totals(): return lax.psum(partial_value, 'seq')  242 us
    psum x1, waiting for transfers between devices, body(): kernel_sum, norm_sum = lax.psum((kernel_part, norm_parts), ('seq', 'dp'))  177 us
    convert_element_type x2, other arithmetic, section_backward(): input_grad = (upstream_grad.astype(jnp.float32) + depthwise_back(padded_g...  43.5 us
    reduce_sum x2, other arithmetic, section_forward(): jnp.sum(conv_out, axis=1)  40.3 us
  transfers between devices with their start and end apart: 44, of which 6 were waited for; matrix products, arithmetic and copies ran while one was open for 5% of the time, Pallas kernels for 0%

commit v1 on v0

v1 whole, which is shorter than its diff:
```python
import types

import jax
import jax.numpy as jnp
from jax import lax
from jax.experimental import pallas as pl
from jax.experimental.pallas import tpu as pltpu
from jax.sharding import PartitionSpec as P

EPSILON = 1e-05
MESH = pl.DeviceIdType.MESH
F32, BF16 = jnp.float32, jnp.bfloat16
D, HALF, ROWS, TAPS, RIM, UTTS = 1536, 768, 256, 32, 16, 32
LANE, TILES = 128, 6
NX, NY, NZ = 4, 4, 8
SEQ = NX * NZ
BLOCK = 12
STEP, GROUP = 32, 3
PADDED = ROWS + 2 * RIM

PLANE = [(dx, dy) for dx in range(NX) for dy in range(NY)]
OFFSETS = [(s, rel) for s in (-2, -1, 0, 1, 2) for rel in (0, 1) if (s, rel) != (0, 0)]
GATHER = [(dx, dy, rel) for dx, dy in PLANE for rel in (0, 1) if (dx, dy, rel) != (0, 0, 0)]


def scratch():
    vm, dma = pltpu.VMEM, pltpu.SemaphoreType.DMA
    return dict(
        hb=vm((ROWS, HALF), BF16),
        gbuf=vm((2, 2, ROWS, HALF), BF16),
        w=vm((2, HALF, D), BF16),
        pst=vm((2, TILES, 40, LANE), F32),
        pb=vm((2, TILES, 40, LANE), F32),
        seg=vm((PADDED, LANE), F32),
        cnt=vm((8, LANE), F32),
        perm=vm((2, HALF, HALF), BF16),
        xf=vm((2, TILES, PADDED, LANE), F32),
        y=vm((2, TILES, ROWS, LANE), F32),
        inv=vm((2, ROWS, LANE), F32),
        act=vm((2, ROWS, HALF), BF16),
        ag=vm((ROWS, HALF), F32),
        cg=vm((TILES, PADDED, LANE), F32),
        kga=vm((TILES, TAPS, 8, LANE), F32),
        gba=vm((2, 2, TILES, 8, LANE), F32),
        halo=vm((4, 2, RIM, HALF), BF16),
        edge=vm((2, 2, RIM, HALF), BF16),
        hx=vm((2, ROWS, HALF), BF16),
        h1=vm((ROWS, HALF), BF16),
        tab=vm((4, 8, LANE), F32),
        tabr=vm((4, 9, 8, LANE), F32),
        gwb=vm((2, 2, HALF, HALF), BF16),
        r1=vm((2, 2, 3, HALF // 4, HALF), BF16),
        s2=vm((2, 2, HALF // 4, HALF), BF16),
        r2=vm((2, 2, 3, HALF // 16, HALF), BF16),
        t3=vm((HALF // 16 + 8, HALF), F32),
        s3=vm((2, 4, 2, 16, HALF), BF16),
        r3=vm((NZ, 2, 16, HALF), BF16),
        sb=vm((16, 32, LANE), F32),
        ar=vm((15, 32, LANE), F32),
        zb=vm((NZ, 32, LANE), F32),
        fs=vm((2, 16, LANE), F32),
        fin=vm((2, 16, 16, LANE), F32),
        lsem=dma((4,)),
        hs=dma((4, 2)), hr=dma((4, 2)),
        ws=dma((2,)), wr=dma((2,)),
        xs=dma((2,)), xr=dma((2,)),
        ts=dma((4, 9)), tr=dma((4, 9)),
        s1s=dma((2, 2, 3)), s1r=dma((2, 2, 3)),
        s2s=dma((2, 2, 3)), s2r=dma((2, 2, 3)),
        s3s=dma((2, 4)), s3r=dma((NZ,)),
        as_=dma((15,)), ar_=dma((15,)),
        zs=dma((7,)), zr=dma((7,)),
        gs=dma((31,)), gr=dma((31,)),
    )


def fold(v):
    total = v[0:8]
    for r in range(8, v.shape[0], 8):
        total = total + v[r : r + 8]
    return total


def dot(a, b):
    return jnp.dot(a, b, preferred_element_type=F32)


def dot_t(a, b):
    return lax.dot_general(a, b, (((1,), (1,)), ((), ())), preferred_element_type=F32)


def cols(c):
    return slice(c * LANE, (c + 1) * LANE)


def main_kernel(names, hid, up, len_ref, w_hbm, ker_ref, gain_ref, bias_ref,
                gi_ref, gw_ref, gk_ref, gg_ref, gb_ref, *refs):
    S = types.SimpleNamespace(**dict(zip(names, refs)))
    i, p, y = lax.axis_index("seq"), lax.axis_index("pipe"), lax.axis_index("dp")
    q = 1 - p
    z, x = lax.div(i, NX), lax.rem(i, NX)
    own_col = pl.multiple_of(p * HALF, HALF)
    oth_col = pl.multiple_of(q * HALF, HALF)

    def dev(seq, pipe, dp):
        return {"seq": seq, "pipe": pipe, "dp": dp}

    def along(offset, pipe):
        return dev(lax.rem(i + offset + SEQ, SEQ), pipe, y)

    def plane(dx, dy, pipe):
        return dev(z * NX + lax.rem(x + dx, NX), pipe, lax.rem(y + dy, NY))

    def depth(dz, pipe):
        return dev(lax.rem(z + dz, NZ) * NX + x, pipe, y)

    core = (p, q)
    sends = []

    def push(src, dst, ssem, rsem, target):
        copy = pltpu.make_async_remote_copy(
            src_ref=src, dst_ref=dst, send_sem=ssem, recv_sem=rsem,
            device_id=target, device_id_type=MESH,
        )
        copy.start()
        sends.append(copy)
        return copy

    loc = [
        pltpu.make_async_copy(hid.at[0, :, pl.ds(own_col, HALF)], S.hb, S.lsem.at[0]),
        pltpu.make_async_copy(w_hbm.at[0, pl.ds(own_col, HALF), :], S.w.at[p], S.lsem.at[1]),
        pltpu.make_async_copy(up.at[0, :, pl.ds(0, HALF)], S.gbuf.at[1, 0], S.lsem.at[2]),
        pltpu.make_async_copy(up.at[0, :, pl.ds(HALF, HALF)], S.gbuf.at[1, 1], S.lsem.at[3]),
    ]
    for copy in loc:
        copy.start()

    barrier = pltpu.get_barrier_semaphore()
    partners = [along(s, core[rel]) for s, rel in OFFSETS]
    partners += [plane(dx, dy, c) for dx, dy in PLANE if (dx, dy) != (0, 0) for c in core]
    partners += [depth(dz, c) for dz in range(1, NZ) for c in core]
    for target in partners:
        pl.semaphore_signal(barrier, inc=1, device_id=target, device_id_type=MESH)

    for h in range(2):
        for c in range(TILES):
            at = slice(h * HALF + c * LANE, h * HALF + (c + 1) * LANE)
            S.pst[h, c, 0:TAPS, :] = ker_ref[0, :, at]
            row = lax.broadcasted_iota(jnp.int32, (8, LANE), 0)
            S.pst[h, c, TAPS:40, :] = jnp.where(
                row == 0, gain_ref[:, at], jnp.where(row == 1, bias_ref[:, at], 0.0)
            )
    for c in range(TILES):
        S.pb[p, c] = S.pst[p, c]

    lens = len_ref[...].astype(F32)
    io0 = lax.broadcasted_iota(jnp.int32, (UTTS, UTTS), 0)
    io1 = lax.broadcasted_iota(jnp.int32, (UTTS, UTTS), 1)
    lens_col = jnp.sum(jnp.where(io0 == io1, lens, 0.0), axis=1, keepdims=True)
    starts = jnp.sum(jnp.where(io0 < io1, lens_col, 0.0), axis=0, keepdims=True)
    bin_total = jnp.sum(lens, axis=1, keepdims=True)
    frame = (lax.broadcasted_iota(jnp.int32, (PADDED, UTTS), 0) + (i * ROWS - RIM)).astype(F32)
    owner = jnp.sum(jnp.where(starts <= frame, 1.0, 0.0), axis=1, keepdims=True) - 1.0
    inside = (frame[:, 0:1] >= 0.0) & (frame[:, 0:1] < bin_total)
    S.seg[...] = jnp.broadcast_to(jnp.where(inside, owner, -2.0), (PADDED, LANE))
    S.cnt[...] = jnp.full((8, LANE), float(D), F32)
    S.cnt[0:1, 0:UTTS] = lens * float(D)

    r = lax.broadcasted_iota(jnp.int32, (HALF, LANE), 0).astype(F32)
    blk = jnp.floor((r + 0.5) / BLOCK)
    word = r - BLOCK * blk
    b4 = jnp.floor((blk + 0.5) / 4.0)
    dig0 = blk - 4.0 * b4
    dig2 = jnp.floor((b4 + 0.5) / 4.0)
    dig1 = b4 - 4.0 * dig2
    lane = lax.broadcasted_iota(jnp.int32, (HALF, LANE), 1).astype(F32)
    for path, (yy, xx) in enumerate(((dig2, dig1), (dig1, dig2))):
        nat = ((dig0 * 4.0 + xx) * 4.0 + yy) * BLOCK + word
        for c in range(TILES):
            S.perm[path, :, cols(c)] = jnp.where(nat == lane + float(c * LANE), 1.0, 0.0).astype(BF16)

    S.kga[...] = jnp.zeros(S.kga.shape, F32)
    S.sb[15] = jnp.zeros((32, LANE), F32)
    S.t3[HALF // 16 :, :] = jnp.zeros((8, HALF), F32)

    pl.semaphore_wait(barrier, len(partners))

    def send_halo(rnd, first, last):
        return [
            push(last, S.halo.at[rnd, 0], S.hs.at[rnd, 0], S.hr.at[rnd, 0], along(1, p)),
            push(first, S.halo.at[rnd, 1], S.hs.at[rnd, 1], S.hr.at[rnd, 1], along(-1, p)),
        ]

    def take_halo(rnd, copies, dst):
        for copy in copies:
            copy.wait_recv()
        for c in range(TILES):
            dst[c, 0:RIM, :] = S.halo[rnd, 0, :, cols(c)].astype(F32)
            dst[c, RIM + ROWS :, :] = S.halo[rnd, 1, :, cols(c)].astype(F32)

    halo_copies = send_halo(
        0,
        hid.at[0, pl.ds(0, RIM), pl.ds(own_col, HALF)],
        hid.at[0, pl.ds(ROWS - RIM, RIM), pl.ds(own_col, HALF)],
    )
    par_copy = push(S.pst.at[q], S.pb.at[p], S.ws.at[0], S.wr.at[0], along(0, q))
    w_copy = push(
        w_hbm.at[0, pl.ds(oth_col, HALF), :], S.w.at[p], S.ws.at[1], S.wr.at[1], along(0, q)
    )

    loc[0].wait()
    for c in range(TILES):
        S.xf[0, c, RIM : RIM + ROWS, :] = S.hb[:, cols(c)].astype(F32)

    steps = ROWS // STEP
    lane_id = lax.broadcasted_iota(jnp.int32, (STEP, LANE), 1).astype(F32)

    def base_of(b):
        return pl.multiple_of(b * STEP, STEP)

    def member(base):
        return S.seg[pl.ds(base + RIM, STEP), :] == lane_id

    def table_add(onehot, v):
        return fold(jnp.where(onehot, jnp.sum(v, axis=1, keepdims=True), 0.0))

    def pick(onehot, row):
        return jnp.sum(jnp.where(onehot, row, 0.0), axis=1, keepdims=True)

    zero_tab = jnp.zeros((8, LANE), F32)

    def send_table(rnd, t1, t2):
        row = lax.broadcasted_iota(jnp.int32, (8, LANE), 0)
        t1 = jnp.sum(t1, axis=0, keepdims=True)
        t2 = jnp.sum(t2, axis=0, keepdims=True)
        S.tab[rnd] = jnp.where(row == 0, t1, jnp.where(row == 1, t2, 0.0))
        return [
            push(S.tab.at[rnd], S.tabr.at[rnd, n], S.ts.at[rnd, n], S.tr.at[rnd, n], along(s, core[rel]))
            for n, (s, rel) in enumerate(OFFSETS)
        ]

    def take_table(rnd, copies):
        total = S.tab[rnd]
        for copy in copies:
            copy.wait_recv()
        for n in range(9):
            total = total + S.tabr[rnd, n]
        count = S.cnt[0:1, :]
        return total[0:1] / count, total[1:2] / count

    def conv_forward(s):
        def step(b, carry):
            t1, t2 = carry
            base = base_of(b)
            centre = S.seg[pl.ds(base + RIM, STEP), :]
            first = second = jnp.zeros((STEP, LANE), F32)
            for g in range(0, TILES, GROUP):
                acc = [jnp.zeros((STEP, LANE), F32) for _ in range(GROUP)]
                for j in range(TAPS):
                    same = S.seg[pl.ds(base + j + 1, STEP), :] == centre
                    for c in range(GROUP):
                        window = S.xf[s, g + c, pl.ds(base + j + 1, STEP), :]
                        acc[c] = acc[c] + jnp.where(same, window * S.pb[s, g + c, j : j + 1, :], 0.0)
                for c in range(GROUP):
                    S.y[s, g + c, pl.ds(base, STEP), :] = acc[c]
                    first = first + acc[c]
                    second = second + acc[c] * acc[c]
            onehot = member(base)
            return t1 + table_add(onehot, first), t2 + table_add(onehot, second)

        return lax.fori_loop(0, steps, step, (zero_tab, zero_tab))

    def moments(rnd, copies):
        mean, square = take_table(rnd, copies)
        spread = jnp.maximum(square - mean * mean, 0.0)
        return mean, lax.rsqrt(spread + EPSILON)

    def normalize(s, base, onehot, mean, scale):
        m, v = pick(onehot, mean), pick(onehot, scale)
        S.inv[s, pl.ds(base, STEP), :] = jnp.broadcast_to(v, (STEP, LANE))
        return m, v

    def activate(s, base, c, normed):
        gain, bias = S.pb[s, c, TAPS : TAPS + 1, :], S.pb[s, c, TAPS + 1 : TAPS + 2, :]
        pre = normed * gain + bias
        sig = jax.nn.sigmoid(pre)
        return gain, pre, sig

    take_halo(0, halo_copies, S.xf.at[0])
    par_copy.wait_recv()
    copies = send_table(0, *conv_forward(0))
    mean, scale = moments(0, copies)

    def norm_step(b, _):
        base = base_of(b)
        m, v = normalize(0, base, member(base), mean, scale)
        for c in range(TILES):
            normed = (S.y[0, c, pl.ds(base, STEP), :] - m) * v
            S.y[0, c, pl.ds(base, STEP), :] = normed
            _, pre, sig = activate(0, base, c, normed)
            S.act[0, pl.ds(base, STEP), cols(c)] = (pre * sig).astype(BF16)
        return 0

    lax.fori_loop(0, steps, norm_step, 0)
    loc[1].wait()
    w_copy.wait_recv()
    S.hx[0] = dot(S.act[0], S.w[0, :, pl.ds(oth_col, HALF)]).astype(BF16)
    copy = push(S.hx.at[0], S.hx.at[1], S.xs.at[0], S.xr.at[0], along(0, q))
    S.ag[...] = dot(S.act[0], S.w[0, :, pl.ds(own_col, HALF)])
    copy.wait_recv()

    def out_step(b, _):
        base = base_of(b)
        at = pl.ds(base, STEP)
        S.h1[at, :] = (S.hb[at, :].astype(F32) + (S.ag[at, :] + S.hx[1, at, :].astype(F32))).astype(BF16)
        return 0

    lax.fori_loop(0, steps, out_step, 0)
    halo_copies = send_halo(1, S.h1.at[pl.ds(0, RIM), :], S.h1.at[pl.ds(ROWS - RIM, RIM), :])
    for c in range(TILES):
        S.xf[1, c, RIM : RIM + ROWS, :] = S.h1[:, cols(c)].astype(F32)
    take_halo(1, halo_copies, S.xf.at[1])

    copies = send_table(1, *conv_forward(1))

    def act_grad(s):
        S.ag[...] = dot_t(S.gbuf[s, 0], S.w[s, :, 0:HALF]) + dot_t(S.gbuf[s, 1], S.w[s, :, HALF:])

    loc[2].wait()
    loc[3].wait()
    act_grad(1)
    mean, scale = moments(1, copies)

    def pre_grad(s, mean, scale):
        def step(b, carry):
            t1, t2, gains, biases = carry
            base = base_of(b)
            onehot = member(base)
            at = pl.ds(base, STEP)
            if s == 1:
                m, v = normalize(1, base, onehot, mean, scale)
            first = second = jnp.zeros((STEP, LANE), F32)
            new_gains, new_biases = [], []
            for c in range(TILES):
                normed = S.y[s, c, at, :]
                if s == 1:
                    normed = (normed - m) * v
                    S.y[1, c, at, :] = normed
                gain, pre, sig = activate(s, base, c, normed)
                if s == 1:
                    S.act[1, at, cols(c)] = (pre * sig).astype(BF16)
                grad = S.ag[at, cols(c)] * sig * (1.0 + pre * (1.0 - sig))
                scaled = grad * gain
                S.ag[at, cols(c)] = scaled
                first = first + scaled
                second = second + scaled * normed
                new_gains.append(gains[c] + fold(grad * normed))
                new_biases.append(biases[c] + fold(grad))
            return (t1 + table_add(onehot, first), t2 + table_add(onehot, second),
                    tuple(new_gains), tuple(new_biases))

        zeros = tuple(zero_tab for _ in range(TILES))
        t1, t2, gains, biases = lax.fori_loop(0, steps, step, (zero_tab, zero_tab, zeros, zeros))
        for c in range(TILES):
            S.gba[s, 0, c] = gains[c]
            S.gba[s, 1, c] = biases[c]
        return t1, t2

    def conv_grad(s, rnd, copies):
        mean_a, mean_b = take_table(rnd, copies)

        def step(b, _):
            base = base_of(b)
            onehot = member(base)
            ca, cb = pick(onehot, mean_a), pick(onehot, mean_b)
            at = pl.ds(base, STEP)
            v = S.inv[s, at, :]
            for c in range(TILES):
                S.cg[c, pl.ds(base + RIM, STEP), :] = v * (S.ag[at, cols(c)] - ca - S.y[s, c, at, :] * cb)
            return 0

        lax.fori_loop(0, steps, step, 0)
        for c in range(TILES):
            S.edge[s, 0, :, cols(c)] = S.cg[c, RIM : 2 * RIM, :].astype(BF16)
            S.edge[s, 1, :, cols(c)] = S.cg[c, ROWS : ROWS + RIM, :].astype(BF16)
        return send_halo(rnd, S.edge.at[s, 0], S.edge.at[s, 1])

    def conv_backward(s):
        def step(b, _):
            base = base_of(b)
            at = pl.ds(base, STEP)
            centre = S.seg[pl.ds(base + RIM, STEP), :]
            for g in range(0, TILES, GROUP):
                acc = [jnp.zeros((STEP, LANE), F32) for _ in range(GROUP)]
                mine = [S.xf[s, g + c, pl.ds(base + RIM, STEP), :] for c in range(GROUP)]
                for j in range(TAPS):
                    same = S.seg[pl.ds(base + TAPS - 1 - j, STEP), :] == centre
                    for c in range(GROUP):
                        window = jnp.where(same, S.cg[g + c, pl.ds(base + TAPS - 1 - j, STEP), :], 0.0)
                        acc[c] = acc[c] + window * S.pb[s, g + c, j : j + 1, :]
                        S.kga[g + c, j] += fold(window * mine[c])
                for c in range(GROUP):
                    passed = S.gbuf[s, p, at, cols(g + c)].astype(F32) + acc[c]
                    if s == 1:
                        S.gbuf[0, p, at, cols(g + c)] = passed.astype(BF16)
                    else:
                        gi_ref[0, at, cols(g + c)] = passed.astype(BF16)
            return 0

        lax.fori_loop(0, steps, step, 0)

    def keep_small(s):
        row = lax.broadcasted_iota(jnp.int32, (8, LANE), 0)
        for c in range(TILES):
            for k in range(4):
                t = c * 5 + k
                at = slice(s * 16 + (t % 2) * 8, s * 16 + (t % 2) * 8 + 8)
                S.sb[t // 2, at, :] = jnp.sum(S.kga[c, 8 * k : 8 * k + 8], axis=1)
            t = c * 5 + 4
            at = slice(s * 16 + (t % 2) * 8, s * 16 + (t % 2) * 8 + 8)
            gsum = jnp.sum(S.gba[s, 0, c], axis=0, keepdims=True)
            bsum = jnp.sum(S.gba[s, 1, c], axis=0, keepdims=True)
            S.sb[t // 2, at, :] = jnp.where(row == 0, gsum, jnp.where(row == 1, bsum, 0.0))

    def weight_partial(s):
        def step(k, _):
            at = pl.ds(pl.multiple_of(k * 256, 256), 256)
            for path in range(2):
                turned = dot_t(S.perm[path, at, :], S.act[s]).astype(BF16)
                S.gwb[s, path, at, :] = dot(turned, S.gbuf[s, path]).astype(BF16)
            return 0

        lax.fori_loop(0, HALF // 256, step, 0)

    def ring_target(path, d):
        return plane(0, d, p) if path == 0 else plane(d, 0, p)

    def ring_index(path, d):
        return lax.rem((y if path == 0 else x) + d, 4)

    q1, q2 = HALF // 4, HALF // 16

    def first_exchange(s):
        return [
            push(
                S.gwb.at[s, path, pl.ds(pl.multiple_of(ring_index(path, d) * q1, q1), q1), :],
                S.r1.at[s, path, d - 1], S.s1s.at[s, path, d - 1], S.s1r.at[s, path, d - 1],
                ring_target(path, d),
            )
            for d in (1, 2, 3) for path in range(2)
        ]

    def second_exchange(s, copies):
        for copy in copies:
            copy.wait_recv()
        for path in range(2):
            def step(k, _):
                at = pl.ds(pl.multiple_of(k * 48, 48), 48)
                mine = pl.ds(pl.multiple_of(ring_index(path, 0) * q1 + k * 48, 48), 48)
                total = S.gwb[s, path, mine, :].astype(F32)
                for d in range(3):
                    total = total + S.r1[s, path, d, at, :].astype(F32)
                S.s2[s, path, at, :] = total.astype(BF16)
                return 0

            lax.fori_loop(0, 4, step, 0)
        return [
            push(
                S.s2.at[s, path, pl.ds(pl.multiple_of(ring_index(1 - path, d) * q2, q2), q2), :],
                S.r2.at[s, path, d - 1], S.s2s.at[s, path, d - 1], S.s2r.at[s, path, d - 1],
                ring_target(1 - path, d),
            )
            for d in (1, 2, 3) for path in range(2)
        ]

    near = lax.div(z, 4) == p

    def third_exchange(s, copies):
        for copy in copies:
            copy.wait_recv()
        for path in range(2):
            mine = pl.ds(pl.multiple_of(ring_index(1 - path, 0) * q2, q2), q2)
            total = S.s2[s, path, mine, :].astype(F32)
            for d in range(3):
                total = total + S.r2[s, path, d].astype(F32)
            S.t3[0:q2, :] = total
            for k in range(4):
                S.s3[s, k, path] = S.t3[BLOCK * k : BLOCK * k + 16, :].astype(BF16)
        for k in range(4):
            target_z = 4 * p + k
            stays = (target_z == z) & (p == s)
            copy = pltpu.make_async_remote_copy(
                src_ref=S.s3.at[s, k], dst_ref=S.r3.at[z], send_sem=S.s3s.at[s, k],
                recv_sem=S.s3r.at[z], device_id=dev(target_z * NX + x, s, y), device_id_type=MESH,
            )

            @pl.when(jnp.logical_not(stays))
            def _():
                copy.start()

            @pl.when(stays)
            def _():
                S.r3[z] = S.s3[s, k]

    def finish_third():
        for s in range(2):
            for k in range(4):
                target_z = 4 * p + k
                stays = (target_z == z) & (p == s)

                @pl.when(jnp.logical_not(stays))
                def _():
                    pltpu.make_async_remote_copy(
                        src_ref=S.s3.at[s, k], dst_ref=S.r3.at[z], send_sem=S.s3s.at[s, k],
                        recv_sem=S.s3r.at[z], device_id=dev(target_z * NX + x, s, y),
                        device_id_type=MESH,
                    ).wait_send()
        for k in range(NZ):
            @pl.when(jnp.logical_not((z == k) & near))
            def _():
                pltpu.make_async_remote_copy(
                    src_ref=S.s3.at[0, 0], dst_ref=S.r3.at[k], send_sem=S.s3s.at[0, 0],
                    recv_sem=S.s3r.at[k], device_id=along(0, q), device_id_type=MESH,
                ).wait_recv()
        for path in range(2):
            total = S.r3[0, path].astype(F32)
            for k in range(1, NZ):
                total = total + S.r3[k, path].astype(F32)
            gw_ref[0, :, path * HALF : (path + 1) * HALF] = total[0:BLOCK]

    copies = send_table(2, *pre_grad(1, mean, scale))
    weight_partial(1)
    halo_copies = conv_grad(1, 2, copies)
    first1 = first_exchange(1)
    take_halo(2, halo_copies, S.cg)
    conv_backward(1)
    copy = push(S.gbuf.at[0, p], S.gbuf.at[0, p], S.xs.at[1], S.xr.at[1], along(0, q))
    keep_small(1)
    S.kga[...] = jnp.zeros(S.kga.shape, F32)
    copy.wait_recv()

    act_grad(0)
    copies = send_table(3, *pre_grad(0, None, None))
    second1 = second_exchange(1, first1)
    weight_partial(0)
    halo_copies = conv_grad(0, 3, copies)
    first0 = first_exchange(0)
    third_exchange(1, second1)
    take_halo(3, halo_copies, S.cg)
    conv_backward(0)
    keep_small(0)

    place = x * NY + y
    small = [
        push(
            S.sb.at[lax.rem(x + dx, NX) * NY + lax.rem(y + dy, NY)], S.ar.at[n],
            S.as_.at[n], S.ar_.at[n], plane(dx, dy, p),
        )
        for n, (dx, dy) in enumerate(PLANE[1:])
    ]
    second0 = second_exchange(0, first0)
    for copy in small:
        copy.wait_recv()
    total = S.sb[place]
    for n in range(15):
        total = total + S.ar[n]
    S.zb[z] = total
    small = [
        push(S.zb.at[z], S.zb.at[z], S.zs.at[dz - 1], S.zr.at[dz - 1], depth(dz, p))
        for dz in range(1, NZ)
    ]
    third_exchange(0, second0)
    for dz in range(1, NZ):
        from_z = lax.rem(z + NZ - dz, NZ)
        pltpu.make_async_remote_copy(
            src_ref=S.zb.at[from_z], dst_ref=S.zb.at[from_z], send_sem=S.zs.at[dz - 1],
            recv_sem=S.zr.at[dz - 1], device_id=depth(dz, p), device_id_type=MESH,
        ).wait_recv()
    total = S.zb[0]
    for k in range(1, NZ):
        total = total + S.zb[k]
    S.fs[0] = total[0:16]
    S.fs[1] = total[16:32]
    S.fin[p, place] = S.fs[p]
    small = [
        push(S.fs.at[core[rel]], S.fin.at[p, place], S.gs.at[n], S.gr.at[n], plane(dx, dy, core[rel]))
        for n, (dx, dy, rel) in enumerate(GATHER)
    ]
    finish_third()
    for copy in small:
        copy.wait_recv()
    for h in range(2):
        for c in range(TILES):
            at = slice(h * HALF + c * LANE, h * HALF + (c + 1) * LANE)
            for k in range(4):
                t = c * 5 + k
                gk_ref[0, 8 * k : 8 * k + 8, at] = S.fin[h, t // 2, (t % 2) * 8 : (t % 2) * 8 + 8, :]
            t = c * 5 + 4
            gg_ref[:, at] = S.fin[h, t // 2, (t % 2) * 8 : (t % 2) * 8 + 1, :]
            gb_ref[:, at] = S.fin[h, t // 2, (t % 2) * 8 + 1 : (t % 2) * 8 + 2, :]
    for copy in sends:
        copy.wait_send()


def body(*args):
    shapes = scratch()
    names = list(shapes)
    vmem, hbm = pl.BlockSpec(memory_space=pltpu.VMEM), pl.BlockSpec(memory_space=pl.ANY)

    def kern(*refs):
        main_kernel(names, *refs)

    return pl.pallas_call(
        kern,
        out_shape=(
            jax.ShapeDtypeStruct((1, ROWS, HALF), BF16),
            jax.ShapeDtypeStruct((1, BLOCK, D), F32),
            jax.ShapeDtypeStruct((1, TAPS, D), F32),
            jax.ShapeDtypeStruct((1, D), F32),
            jax.ShapeDtypeStruct((1, D), F32),
        ),
        in_specs=[hbm, hbm, vmem, hbm, vmem, vmem, vmem],
        out_specs=[vmem] * 5,
        scratch_shapes=list(shapes.values()),
        compiler_params=pltpu.CompilerParams(
            collective_id=0, has_side_effects=True, vmem_limit_bytes=56 << 20
        ),
    )(*args)


def solution(mesh):
    return jax.shard_map(
        body,
        mesh=mesh,
        in_specs=(
            P("dp", "seq", None),
            P("dp", "seq", None),
            P("dp", None),
            P("pipe", None, None),
            P("pipe", None, None),
            P("pipe", None),
            P("pipe", None),
        ),
        out_specs=(
            P("dp", "seq", "pipe"),
            P("pipe", ("seq", "dp"), None),
            P("pipe", None, None),
            P("pipe", None),
            P("pipe", None),
        ),
        check_vma=False,
    )
```

time: 1950 us -> 115 us (0.06)
  blocking collectives: 1190 us -> 0 us
  starting transfers between devices: 327 us -> 0 us
  waiting for transfers between devices: 201 us -> 0 us
  other arithmetic: 117 us -> 0 us
  Pallas kernels: 0 us -> 107 us
  local copies, waits for them, and re-layouts: 48.1 us -> 7.55 us
  matrix products: 34.3 us -> 0 us
    psum x5 -> x0, blocking collectives: 813 us -> none  [the longest x1 571 us: body(): kernel_sum, norm_sum = lax.psum((kernel_part, norm_parts), ('seq', 'dp'))]
    unnamed x1 -> x0, blocking collectives: 382 us -> none
    unnamed x32 -> x0, starting transfers between devices: 276 us -> none
    psum x1 -> x0, waiting for transfers between devices: 177 us -> none  [body(): kernel_sum, norm_sum = lax.psum((kernel_part, norm_parts), ('seq', 'dp'))]
    pallas_call x0 -> x1, Pallas kernels: none -> 107 us  [body(): pl.pallas_call(kern, out_shape=(jax.ShapeDtypeStruct((1, ROWS, HALF), BF1...]
    reduce_sum x8 -> x0, other arithmetic: 61.6 us -> none  [the longest x2 40.3 us: section_forward(): jnp.sum(conv_out, axis=1)]
    ppermute x11 -> x0, starting transfers between devices: 50.8 us -> none  [the longest x3 36.2 us: from_behind(): return lax.ppermute(x, axis, pairs)]
    convert_element_type x3 -> x0, other arithmetic: 45.8 us -> none  [the longest x2 43.5 us: section_backward(): input_grad = (upstream_grad.astype(jnp.float32) + depthwise_back(padded_g...]
  transfers between devices with their start and end apart: 44 -> 0, of which waited for: 6 -> 0; matrix products, arithmetic and copies ran while one was open for 5% -> 0% of each run, Pallas kernels for 0% -> 0%
where the time goes in v1:
time: 115 us
  Pallas kernels  107 us (93%)
  local copies, waits for them, and re-layouts  7.55 us (7%)
    pallas_call x1, Pallas kernels, body(): pl.pallas_call(kern, out_shape=(jax.ShapeDtypeStruct((1, ROWS, HALF), BF1...  107 us
    unnamed x4, local copies, waits for them, and re-layouts  5.95 us

profile of v1, /device:TPU:1, one launch (start us, length us, event | category | flops | bytes accessed | tf_op | source)
XLA Modules:
  0.0 115.1 jit_solution(2710418101406438412)
XLA Ops:
  0.6 106.9 %shard_map.110 = (bf16[1,256,768]{2,1,0:T(8,128)(2,1)}, f32[1,12,1536]{2,1,0:T(8,128)}, f32[1,32,1536]{2,1,0:T(8,128)}, f32[1,1536]{1,0:T(1,128)}, f32[1,1536]{1,0:T(1,128)}) custom-call(bf16[1,256,1536]{2,1,0:T(8,128)(2,1)} %refs_0_.1, bf16[1,256,1536]{2,1,0:T(8,128)(2,1)} %refs_1_.1, s32[1,32]{1,0:T(1,128)} %refs_2_.1, bf16[1,1536,1536]{2,1,0:T(8,128)(2,1)} %refs_3_.1, ...), custom_call_target="tpu_custom_call" | custom-call | tf_op jit(solution)/shard_map/pallas_call | solution.py:613
  107.5 1.6 %copy.12 = f32[1,12,1536]{2,0,1:T(1,128)} copy(f32[1,12,1536]{2,1,0:T(8,128)} %get-tuple-element.6) | data formatting | bytes 147456 | tf_op jit(solution)/shard_map/pallas_call | solution.py:613
  109.2 1.8 %copy.17 = bf16[1,256,768]{2,1,0:T(8,128)(2,1)} copy(bf16[1,256,768]{2,1,0:T(8,128)(2,1)} %get-tuple-element.15) | data formatting | bytes 786432
  110.9 1.6 %copy.18 = f32[1,32,1536]{2,1,0:T(8,128)} copy(f32[1,32,1536]{2,1,0:T(8,128)} %get-tuple-element.17) | data formatting | bytes 393216
  112.5 1.3 %copy.19 = f32[1,1536]{1,0:T(1,128)} copy(f32[1,1536]{1,0:T(1,128)} %get-tuple-element.18) | data formatting | bytes 12288
  113.8 1.3 %copy.20 = f32[1,1536]{1,0:T(1,128)} copy(f32[1,1536]{1,0:T(1,128)} %get-tuple-element.19) | data formatting | bytes 12288

commit v2 on v1

--- a/solution.py
+++ b/solution.py
@@ -40,7 +40,7 @@
         act=vm((2, ROWS, HALF), BF16),
         ag=vm((ROWS, HALF), F32),
         cg=vm((TILES, PADDED, LANE), F32),
-        kga=vm((TILES, TAPS, 8, LANE), F32),
+        kga=vm((2, TILES, TAPS, 8, LANE), F32),
         gba=vm((2, 2, TILES, 8, LANE), F32),
         halo=vm((4, 2, RIM, HALF), BF16),
         edge=vm((2, 2, RIM, HALF), BF16),
@@ -248,7 +248,12 @@
         count = S.cnt[0:1, :]
         return total[0:1] / count, total[1:2] / count
 
-    def conv_forward(s):
+    def inside_first(step, carry, then):
+        carry = lax.fori_loop(1, steps - 1, step, carry)
+        then()
+        return lax.fori_loop(0, 2, lambda b, held: step(b * (steps - 1), held), carry)
+
+    def conv_forward(s, copies):
         def step(b, carry):
             t1, t2 = carry
             base = base_of(b)
@@ -268,7 +273,7 @@
             onehot = member(base)
             return t1 + table_add(onehot, first), t2 + table_add(onehot, second)
 
-        return lax.fori_loop(0, steps, step, (zero_tab, zero_tab))
+        return inside_first(step, (zero_tab, zero_tab), lambda: take_halo(s, copies, S.xf.at[s]))
 
     def moments(rnd, copies):
         mean, square = take_table(rnd, copies)
@@ -286,9 +291,8 @@
         sig = jax.nn.sigmoid(pre)
         return gain, pre, sig
 
-    take_halo(0, halo_copies, S.xf.at[0])
     par_copy.wait_recv()
-    copies = send_table(0, *conv_forward(0))
+    copies = send_table(0, *conv_forward(0, halo_copies))
     mean, scale = moments(0, copies)
 
     def norm_step(b, _):
@@ -319,9 +323,8 @@
     halo_copies = send_halo(1, S.h1.at[pl.ds(0, RIM), :], S.h1.at[pl.ds(ROWS - RIM, RIM), :])
     for c in range(TILES):
         S.xf[1, c, RIM : RIM + ROWS, :] = S.h1[:, cols(c)].astype(F32)
-    take_halo(1, halo_copies, S.xf.at[1])
-
-    copies = send_table(1, *conv_forward(1))
+
+    copies = send_table(1, *conv_forward(1, halo_copies))
 
     def act_grad(s):
         S.ag[...] = dot_t(S.gbuf[s, 0], S.w[s, :, 0:HALF]) + dot_t(S.gbuf[s, 1], S.w[s, :, HALF:])
@@ -385,20 +388,18 @@
             S.edge[s, 1, :, cols(c)] = S.cg[c, ROWS : ROWS + RIM, :].astype(BF16)
         return send_halo(rnd, S.edge.at[s, 0], S.edge.at[s, 1])
 
-    def conv_backward(s):
+    def conv_backward(s, then):
         def step(b, _):
             base = base_of(b)
             at = pl.ds(base, STEP)
             centre = S.seg[pl.ds(base + RIM, STEP), :]
             for g in range(0, TILES, GROUP):
                 acc = [jnp.zeros((STEP, LANE), F32) for _ in range(GROUP)]
-                mine = [S.xf[s, g + c, pl.ds(base + RIM, STEP), :] for c in range(GROUP)]
                 for j in range(TAPS):
                     same = S.seg[pl.ds(base + TAPS - 1 - j, STEP), :] == centre
                     for c in range(GROUP):
-                        window = jnp.where(same, S.cg[g + c, pl.ds(base + TAPS - 1 - j, STEP), :], 0.0)
-                        acc[c] = acc[c] + window * S.pb[s, g + c, j : j + 1, :]
-                        S.kga[g + c, j] += fold(window * mine[c])
+                        window = S.cg[g + c, pl.ds(base + TAPS - 1 - j, STEP), :]
+                        acc[c] = acc[c] + jnp.where(same, window * S.pb[s, g + c, j : j + 1, :], 0.0)
                 for c in range(GROUP):
                     passed = S.gbuf[s, p, at, cols(g + c)].astype(F32) + acc[c]
                     if s == 1:
@@ -407,7 +408,22 @@
                         gi_ref[0, at, cols(g + c)] = passed.astype(BF16)
             return 0
 
-        lax.fori_loop(0, steps, step, 0)
+        inside_first(step, 0, then)
+
+    def kernel_grad(s, low, high):
+        def step(b, _):
+            base = base_of(b)
+            centre = S.seg[pl.ds(base + RIM, STEP), :]
+            for g in range(0, TILES, GROUP):
+                mine = [S.cg[g + c, pl.ds(base + RIM, STEP), :] for c in range(GROUP)]
+                for j in range(TAPS):
+                    same = S.seg[pl.ds(base + j + 1, STEP), :] == centre
+                    for c in range(GROUP):
+                        window = S.xf[s, g + c, pl.ds(base + j + 1, STEP), :]
+                        S.kga[s, g + c, j] += fold(jnp.where(same, window * mine[c], 0.0))
+            return 0
+
+        lax.fori_loop(low, high, step, 0)
 
     def keep_small(s):
         row = lax.broadcasted_iota(jnp.int32, (8, LANE), 0)
@@ -415,7 +431,7 @@
             for k in range(4):
                 t = c * 5 + k
                 at = slice(s * 16 + (t % 2) * 8, s * 16 + (t % 2) * 8 + 8)
-                S.sb[t // 2, at, :] = jnp.sum(S.kga[c, 8 * k : 8 * k + 8], axis=1)
+                S.sb[t // 2, at, :] = jnp.sum(S.kga[s, c, 8 * k : 8 * k + 8], axis=1)
             t = c * 5 + 4
             at = slice(s * 16 + (t % 2) * 8, s * 16 + (t % 2) * 8 + 8)
             gsum = jnp.sum(S.gba[s, 0, c], axis=0, keepdims=True)
@@ -526,28 +542,31 @@
             total = S.r3[0, path].astype(F32)
             for k in range(1, NZ):
                 total = total + S.r3[k, path].astype(F32)
-            gw_ref[0, :, path * HALF : (path + 1) * HALF] = total[0:BLOCK]
+            for k in range(BLOCK):
+                gw_ref[k, :, path * HALF : (path + 1) * HALF] = total[k : k + 1]
 
     copies = send_table(2, *pre_grad(1, mean, scale))
     weight_partial(1)
     halo_copies = conv_grad(1, 2, copies)
     first1 = first_exchange(1)
-    take_halo(2, halo_copies, S.cg)
-    conv_backward(1)
+
+    def while_away():
+        kernel_grad(1, 0, 4)
+        take_halo(2, halo_copies, S.cg)
+
+    conv_backward(1, while_away)
     copy = push(S.gbuf.at[0, p], S.gbuf.at[0, p], S.xs.at[1], S.xr.at[1], along(0, q))
-    keep_small(1)
-    S.kga[...] = jnp.zeros(S.kga.shape, F32)
     copy.wait_recv()
 
     act_grad(0)
     copies = send_table(3, *pre_grad(0, None, None))
+    weight_partial(0)
+    kernel_grad(1, 4, steps)
+    keep_small(1)
     second1 = second_exchange(1, first1)
-    weight_partial(0)
     halo_copies = conv_grad(0, 3, copies)
     first0 = first_exchange(0)
-    third_exchange(1, second1)
-    take_halo(3, halo_copies, S.cg)
-    conv_backward(0)
+    kernel_grad(0, 0, steps)
     keep_small(0)
 
     place = x * NY + y
@@ -558,7 +577,8 @@
         )
         for n, (dx, dy) in enumerate(PLANE[1:])
     ]
-    second0 = second_exchange(0, first0)
+    third_exchange(1, second1)
+    conv_backward(0, lambda: take_halo(3, halo_copies, S.cg))
     for copy in small:
         copy.wait_recv()
     total = S.sb[place]
@@ -569,7 +589,7 @@
         push(S.zb.at[z], S.zb.at[z], S.zs.at[dz - 1], S.zr.at[dz - 1], depth(dz, p))
         for dz in range(1, NZ)
     ]
-    third_exchange(0, second0)
+    second0 = second_exchange(0, first0)
     for dz in range(1, NZ):
         from_z = lax.rem(z + NZ - dz, NZ)
         pltpu.make_async_remote_copy(
@@ -586,6 +606,7 @@
         push(S.fs.at[core[rel]], S.fin.at[p, place], S.gs.at[n], S.gr.at[n], plane(dx, dy, core[rel]))
         for n, (dx, dy, rel) in enumerate(GATHER)
     ]
+    third_exchange(0, second0)
     finish_third()
     for copy in small:
         copy.wait_recv()
@@ -602,6 +623,11 @@
         copy.wait_send()
 
 
+def relay_kernel(*refs):
+    for k in range(5):
+        refs[5 + k][...] = refs[k][...]
+
+
 def body(*args):
     shapes = scratch()
     names = list(shapes)
@@ -610,11 +636,11 @@
     def kern(*refs):
         main_kernel(names, *refs)
 
-    return pl.pallas_call(
+    results = pl.pallas_call(
         kern,
         out_shape=(
             jax.ShapeDtypeStruct((1, ROWS, HALF), BF16),
-            jax.ShapeDtypeStruct((1, BLOCK, D), F32),
+            jax.ShapeDtypeStruct((BLOCK, 1, D), F32),
             jax.ShapeDtypeStruct((1, TAPS, D), F32),
             jax.ShapeDtypeStruct((1, D), F32),
             jax.ShapeDtypeStruct((1, D), F32),
@@ -626,6 +652,13 @@
             collective_id=0, has_side_effects=True, vmem_limit_bytes=56 << 20
         ),
     )(*args)
+    gi, gw, gk, gg, gb = pl.pallas_call(
+        relay_kernel,
+        out_shape=tuple(jax.ShapeDtypeStruct(r.shape, r.dtype) for r in results),
+        in_specs=[vmem] * 5,
+        out_specs=[vmem] * 5,
+    )(*results)
+    return gi, gw.reshape(1, BLOCK, D), gk, gg, gb
 
 
 def solution(mesh):

time: 115 us -> 99.3 us (0.86)
  Pallas kernels: 107 us -> 98.5 us
  local copies, waits for them, and re-layouts: 7.55 us -> 0 us
    pallas_call x1, Pallas kernels: 107 us -> 96.6 us  [body(): pl.pallas_call(kern, out_shape=(jax.ShapeDtypeStruct((1, ROWS, HALF), BF1...]
    unnamed x4 -> x0, local copies, waits for them, and re-layouts: 5.95 us -> none
    pallas_call x0 -> x1, Pallas kernels: none -> 1.95 us  [body(): pl.pallas_call(relay_kernel, out_shape=tuple((jax.ShapeDtypeStruct(r.shap...]
    pallas_call x1 -> x0, local copies, waits for them, and re-layouts: 1.6 us -> none  [body(): pl.pallas_call(kern, out_shape=(jax.ShapeDtypeStruct((1, ROWS, HALF), BF1...]
where the time goes in v2:
time: 99.3 us; the launch traced here: 99.2 us
  Pallas kernels  98.5 us (99%)
    pallas_call x1, Pallas kernels, body(): pl.pallas_call(kern, out_shape=(jax.ShapeDtypeStruct((1, ROWS, HALF), BF1...  96.6 us

profile of v2, /device:TPU:1, one launch (start us, length us, event | category | flops | bytes accessed | tf_op | source)
XLA Modules:
  0.0 99.2 jit_solution(15467901156289130616)
XLA Ops:
  0.6 96.6 %shard_map.110 = (bf16[1,256,768]{2,1,0:T(8,128)(2,1)}, f32[12,1,1536]{2,1,0:T(1,128)}, f32[1,32,1536]{2,1,0:T(8,128)}, f32[1,1536]{1,0:T(1,128)}, f32[1,1536]{1,0:T(1,128)}) custom-call(bf16[1,256,1536]{2,1,0:T(8,128)(2,1)} %refs_0_.1, bf16[1,256,1536]{2,1,0:T(8,128)(2,1)} %refs_1_.1, s32[1,32]{1,0:T(1,128)} %refs_2_.1, bf16[1,1536,1536]{2,1,0:T(8,128)(2,1)} %refs_3_.1, ...), custom_call_target="tpu_custom_call" | custom-call | tf_op jit(solution)/shard_map/pallas_call | solution.py:639
  97.2 1.9 %shard_map.111 = (bf16[1,256,768]{2,1,0:T(8,128)(2,1)}, f32[12,1,1536]{2,1,0:T(1,128)}, f32[1,32,1536]{2,1,0:T(8,128)}, f32[1,1536]{1,0:T(1,128)}, f32[1,1536]{1,0:T(1,128)}) custom-call(bf16[1,256,768]{2,1,0:T(8,128)(2,1)} %get-tuple-element.15.refs_0_, f32[12,1,1536]{2,1,0:T(1,128)} %get-tuple-element.16.refs_1_, ...), custom_call_target="tpu_custom_call" | custom-call | tf_op jit(solution)/shard_map/pallas_call | solution.py:655

commit v3 on v2

--- a/solution.py
+++ b/solution.py
@@ -35,25 +35,29 @@
         cnt=vm((8, LANE), F32),
         perm=vm((2, HALF, HALF), BF16),
         xf=vm((2, TILES, PADDED, LANE), F32),
-        y=vm((2, TILES, ROWS, LANE), F32),
+        y=vm((2, TILES, PADDED, LANE), F32),
+        nrm=vm((2, TILES, ROWS, LANE), F32),
+        cb=vm((3, TILES, ROWS, LANE), F32),
         inv=vm((2, ROWS, LANE), F32),
         act=vm((2, ROWS, HALF), BF16),
-        ag=vm((ROWS, HALF), F32),
+        ag=vm((2, ROWS, HALF), F32),
+        part=vm((ROWS, HALF), F32),
         cg=vm((TILES, PADDED, LANE), F32),
         kga=vm((2, TILES, TAPS, 8, LANE), F32),
         gba=vm((2, 2, TILES, 8, LANE), F32),
-        halo=vm((4, 2, RIM, HALF), BF16),
-        edge=vm((2, 2, RIM, HALF), BF16),
+        halo=vm((5, 2, RIM, HALF), BF16),
+        edge=vm((3, 2, RIM, HALF), BF16),
         hx=vm((2, ROWS, HALF), BF16),
         h1=vm((ROWS, HALF), BF16),
         tab=vm((4, 8, LANE), F32),
         tabr=vm((4, 9, 8, LANE), F32),
-        gwb=vm((2, 2, HALF, HALF), BF16),
-        r1=vm((2, 2, 3, HALF // 4, HALF), BF16),
+        turn=vm((2, 2, HALF, ROWS), BF16),
+        ta=vm((2, 4, 2, HALF // 4, ROWS), BF16),
+        gq=vm((2, 3, ROWS, HALF), BF16),
         s2=vm((2, 2, HALF // 4, HALF), BF16),
-        r2=vm((2, 2, 3, HALF // 16, HALF), BF16),
+        r2=vm((2, 3, 2, HALF // 16, HALF), BF16),
         t3=vm((HALF // 16 + 8, HALF), F32),
-        s3=vm((2, 4, 2, 16, HALF), BF16),
+        s3=vm((2, NZ, 16, HALF), BF16),
         r3=vm((NZ, 2, 16, HALF), BF16),
         sb=vm((16, 32, LANE), F32),
         ar=vm((15, 32, LANE), F32),
@@ -61,13 +65,14 @@
         fs=vm((2, 16, LANE), F32),
         fin=vm((2, 16, 16, LANE), F32),
         lsem=dma((4,)),
-        hs=dma((4, 2)), hr=dma((4, 2)),
+        hs=dma((5, 2)), hr=dma((5, 2)),
         ws=dma((2,)), wr=dma((2,)),
         xs=dma((2,)), xr=dma((2,)),
         ts=dma((4, 9)), tr=dma((4, 9)),
-        s1s=dma((2, 2, 3)), s1r=dma((2, 2, 3)),
-        s2s=dma((2, 2, 3)), s2r=dma((2, 2, 3)),
-        s3s=dma((2, 4)), s3r=dma((NZ,)),
+        tas=dma((2, 4, 2)), tar=dma((2, 4, 2)),
+        gqs=dma((2, 3)), gqr=dma((2, 3)),
+        s2s=dma((2, 3)), s2r=dma((2, 3)),
+        s3s=dma((2, NZ)), s3r=dma((NZ, 2)),
         as_=dma((15,)), ar_=dma((15,)),
         zs=dma((7,)), zr=dma((7,)),
         gs=dma((31,)), gr=dma((31,)),
@@ -267,7 +272,7 @@
                         window = S.xf[s, g + c, pl.ds(base + j + 1, STEP), :]
                         acc[c] = acc[c] + jnp.where(same, window * S.pb[s, g + c, j : j + 1, :], 0.0)
                 for c in range(GROUP):
-                    S.y[s, g + c, pl.ds(base, STEP), :] = acc[c]
+                    S.y[s, g + c, pl.ds(base + RIM, STEP), :] = acc[c]
                     first = first + acc[c]
                     second = second + acc[c] * acc[c]
             onehot = member(base)
@@ -291,48 +296,8 @@
         sig = jax.nn.sigmoid(pre)
         return gain, pre, sig
 
-    par_copy.wait_recv()
-    copies = send_table(0, *conv_forward(0, halo_copies))
-    mean, scale = moments(0, copies)
-
-    def norm_step(b, _):
-        base = base_of(b)
-        m, v = normalize(0, base, member(base), mean, scale)
-        for c in range(TILES):
-            normed = (S.y[0, c, pl.ds(base, STEP), :] - m) * v
-            S.y[0, c, pl.ds(base, STEP), :] = normed
-            _, pre, sig = activate(0, base, c, normed)
-            S.act[0, pl.ds(base, STEP), cols(c)] = (pre * sig).astype(BF16)
-        return 0
-
-    lax.fori_loop(0, steps, norm_step, 0)
-    loc[1].wait()
-    w_copy.wait_recv()
-    S.hx[0] = dot(S.act[0], S.w[0, :, pl.ds(oth_col, HALF)]).astype(BF16)
-    copy = push(S.hx.at[0], S.hx.at[1], S.xs.at[0], S.xr.at[0], along(0, q))
-    S.ag[...] = dot(S.act[0], S.w[0, :, pl.ds(own_col, HALF)])
-    copy.wait_recv()
-
-    def out_step(b, _):
-        base = base_of(b)
-        at = pl.ds(base, STEP)
-        S.h1[at, :] = (S.hb[at, :].astype(F32) + (S.ag[at, :] + S.hx[1, at, :].astype(F32))).astype(BF16)
-        return 0
-
-    lax.fori_loop(0, steps, out_step, 0)
-    halo_copies = send_halo(1, S.h1.at[pl.ds(0, RIM), :], S.h1.at[pl.ds(ROWS - RIM, RIM), :])
-    for c in range(TILES):
-        S.xf[1, c, RIM : RIM + ROWS, :] = S.h1[:, cols(c)].astype(F32)
-
-    copies = send_table(1, *conv_forward(1, halo_copies))
-
     def act_grad(s):
-        S.ag[...] = dot_t(S.gbuf[s, 0], S.w[s, :, 0:HALF]) + dot_t(S.gbuf[s, 1], S.w[s, :, HALF:])
-
-    loc[2].wait()
-    loc[3].wait()
-    act_grad(1)
-    mean, scale = moments(1, copies)
+        S.ag[s] = dot_t(S.gbuf[s, 0], S.w[s, :, 0:HALF]) + dot_t(S.gbuf[s, 1], S.w[s, :, HALF:])
 
     def pre_grad(s, mean, scale):
         def step(b, carry):
@@ -345,16 +310,19 @@
             first = second = jnp.zeros((STEP, LANE), F32)
             new_gains, new_biases = [], []
             for c in range(TILES):
-                normed = S.y[s, c, at, :]
                 if s == 1:
-                    normed = (normed - m) * v
-                    S.y[1, c, at, :] = normed
+                    normed = (S.y[1, c, pl.ds(base + RIM, STEP), :] - m) * v
+                    S.nrm[1, c, at, :] = normed
+                else:
+                    normed = S.nrm[0, c, at, :]
                 gain, pre, sig = activate(s, base, c, normed)
                 if s == 1:
                     S.act[1, at, cols(c)] = (pre * sig).astype(BF16)
-                grad = S.ag[at, cols(c)] * sig * (1.0 + pre * (1.0 - sig))
+                grad = S.ag[s, at, cols(c)] * sig * (1.0 + pre * (1.0 - sig))
                 scaled = grad * gain
-                S.ag[at, cols(c)] = scaled
+                S.ag[s, at, cols(c)] = scaled
+                if s == 1:
+                    S.cg[c, pl.ds(base + RIM, STEP), :] = scaled
                 first = first + scaled
                 second = second + scaled * normed
                 new_gains.append(gains[c] + fold(grad * normed))
@@ -369,9 +337,7 @@
             S.gba[s, 1, c] = biases[c]
         return t1, t2
 
-    def conv_grad(s, rnd, copies):
-        mean_a, mean_b = take_table(rnd, copies)
-
+    def conv_grad(s, mean_a, mean_b):
         def step(b, _):
             base = base_of(b)
             onehot = member(base)
@@ -379,14 +345,56 @@
             at = pl.ds(base, STEP)
             v = S.inv[s, at, :]
             for c in range(TILES):
-                S.cg[c, pl.ds(base + RIM, STEP), :] = v * (S.ag[at, cols(c)] - ca - S.y[s, c, at, :] * cb)
+                S.cg[c, pl.ds(base + RIM, STEP), :] = v * (S.ag[s, at, cols(c)] - ca - S.nrm[s, c, at, :] * cb)
             return 0
 
         lax.fori_loop(0, steps, step, 0)
+
+    def send_edges(rnd, k, src):
         for c in range(TILES):
-            S.edge[s, 0, :, cols(c)] = S.cg[c, RIM : 2 * RIM, :].astype(BF16)
-            S.edge[s, 1, :, cols(c)] = S.cg[c, ROWS : ROWS + RIM, :].astype(BF16)
-        return send_halo(rnd, S.edge.at[s, 0], S.edge.at[s, 1])
+            S.edge[k, 0, :, cols(c)] = src[c, RIM : 2 * RIM, :].astype(BF16)
+            S.edge[k, 1, :, cols(c)] = src[c, ROWS : ROWS + RIM, :].astype(BF16)
+        return send_halo(rnd, S.edge.at[k, 0], S.edge.at[k, 1])
+
+    def back_step(k, src):
+        def step(b, _):
+            base = base_of(b)
+            centre = S.seg[pl.ds(base + RIM, STEP), :]
+            for g in range(0, TILES, GROUP):
+                acc = [jnp.zeros((STEP, LANE), F32) for _ in range(GROUP)]
+                for j in range(TAPS):
+                    same = S.seg[pl.ds(base + TAPS - 1 - j, STEP), :] == centre
+                    for c in range(GROUP):
+                        term = S.pb[1, g + c, j : j + 1, :]
+                        if src is not None:
+                            term = src[g + c, pl.ds(base + TAPS - 1 - j, STEP), :] * term
+                        acc[c] = acc[c] + jnp.where(same, term, 0.0)
+                for c in range(GROUP):
+                    S.cb[k, g + c, pl.ds(base, STEP), :] = acc[c]
+            return 0
+
+        return step
+
+    def back_inner(k, src):
+        lax.fori_loop(1, steps - 1, back_step(k, src), 0)
+
+    def back_outer(k, src):
+        lax.fori_loop(0, 2, lambda b, _: back_step(k, src)(b * (steps - 1), 0), 0)
+
+    def pass_down(mean, mean_a, mean_b):
+        def step(b, _):
+            base = base_of(b)
+            onehot = member(base)
+            at = pl.ds(base, STEP)
+            v = S.inv[1, at, :]
+            slope = pick(onehot, mean_b) * v
+            level = pick(onehot, mean_a) - slope * pick(onehot, mean)
+            for c in range(TILES):
+                back = v * (S.cb[2, c, at, :] - level * S.cb[0, c, at, :] - slope * S.cb[1, c, at, :])
+                S.gbuf[0, p, at, cols(c)] = (S.gbuf[1, p, at, cols(c)].astype(F32) + back).astype(BF16)
+            return 0
+
+        lax.fori_loop(0, steps, step, 0)
 
     def conv_backward(s, then):
         def step(b, _):
@@ -402,10 +410,7 @@
                         acc[c] = acc[c] + jnp.where(same, window * S.pb[s, g + c, j : j + 1, :], 0.0)
                 for c in range(GROUP):
                     passed = S.gbuf[s, p, at, cols(g + c)].astype(F32) + acc[c]
-                    if s == 1:
-                        S.gbuf[0, p, at, cols(g + c)] = passed.astype(BF16)
-                    else:
-                        gi_ref[0, at, cols(g + c)] = passed.astype(BF16)
+                    gi_ref[0, at, cols(g + c)] = passed.astype(BF16)
             return 0
 
         inside_first(step, 0, then)
@@ -438,134 +443,180 @@
             bsum = jnp.sum(S.gba[s, 1, c], axis=0, keepdims=True)
             S.sb[t // 2, at, :] = jnp.where(row == 0, gsum, jnp.where(row == 1, bsum, 0.0))
 
-    def weight_partial(s):
+    q1, q2 = HALF // 4, HALF // 16
+    first_place = jnp.where(p == 0, y, x)
+    second_place = jnp.where(p == 0, x, y)
+
+    def first_ring(d, path):
+        return plane(d * path, d * (1 - path), path)
+
+    def second_ring(d):
+        return plane(d * (1 - p), d * p, p)
+
+    def send_cotangent(s):
+        return [
+            push(S.gbuf.at[s, p], S.gq.at[s, d - 1], S.gqs.at[s, d - 1], S.gqr.at[s, d - 1], first_ring(d, p))
+            for d in (1, 3, 2)
+        ]
+
+    def turn_activation(s):
         def step(k, _):
             at = pl.ds(pl.multiple_of(k * 256, 256), 256)
             for path in range(2):
-                turned = dot_t(S.perm[path, at, :], S.act[s]).astype(BF16)
-                S.gwb[s, path, at, :] = dot(turned, S.gbuf[s, path]).astype(BF16)
+                S.turn[s, path, at, :] = dot_t(S.perm[path, at, :], S.act[s]).astype(BF16)
             return 0
 
         lax.fori_loop(0, HALF // 256, step, 0)
 
-    def ring_target(path, d):
-        return plane(0, d, p) if path == 0 else plane(d, 0, p)
-
-    def ring_index(path, d):
-        return lax.rem((y if path == 0 else x) + d, 4)
-
-    q1, q2 = HALF // 4, HALF // 16
-
-    def first_exchange(s):
+    def push_activation(s):
+        copies = []
+        for d in range(4):
+            for rel in range(2):
+                path = core[rel]
+                place = lax.rem(jnp.where(path == 0, y, x) + d, 4)
+                rows = pl.ds(pl.multiple_of(place * q1, q1), q1)
+                if (d, rel) == (0, 0):
+                    S.ta[s, 0, p] = S.turn[s, p, rows, :]
+                else:
+                    copies.append(push(
+                        S.turn.at[s, path, rows, :], S.ta.at[s, d, p], S.tas.at[s, d, rel], S.tar.at[s, d, rel],
+                        first_ring(d, path),
+                    ))
+        return copies
+
+    def first_sum(s, copies):
+        for copy in copies:
+            copy.wait_recv()
+        for h in range(2):
+            total = dot(S.ta[s, 0, h], S.gbuf[s, p])
+            for d in range(3):
+                total = total + dot(S.ta[s, d + 1, h], S.gq[s, d])
+            S.s2[s, h] = total.astype(BF16)
         return [
             push(
-                S.gwb.at[s, path, pl.ds(pl.multiple_of(ring_index(path, d) * q1, q1), q1), :],
-                S.r1.at[s, path, d - 1], S.s1s.at[s, path, d - 1], S.s1r.at[s, path, d - 1],
-                ring_target(path, d),
+                S.s2.at[s, :, pl.ds(pl.multiple_of(lax.rem(second_place + d, 4) * q2, q2), q2), :],
+                S.r2.at[s, d - 1], S.s2s.at[s, d - 1], S.s2r.at[s, d - 1], second_ring(d),
             )
-            for d in (1, 2, 3) for path in range(2)
+            for d in (1, 3, 2)
         ]
 
-    def second_exchange(s, copies):
+    def third_copy(s, dz):
+        rel = jnp.where(p == s, 0, 1)
+        return pltpu.make_async_remote_copy(
+            src_ref=S.s3.at[s, lax.rem(z + dz, NZ)], dst_ref=S.r3.at[dz, rel], send_sem=S.s3s.at[s, dz],
+            recv_sem=S.s3r.at[dz, rel], device_id=depth(dz, s), device_id_type=MESH,
+        )
+
+    def second_sum(s, copies):
         for copy in copies:
             copy.wait_recv()
-        for path in range(2):
-            def step(k, _):
-                at = pl.ds(pl.multiple_of(k * 48, 48), 48)
-                mine = pl.ds(pl.multiple_of(ring_index(path, 0) * q1 + k * 48, 48), 48)
-                total = S.gwb[s, path, mine, :].astype(F32)
-                for d in range(3):
-                    total = total + S.r1[s, path, d, at, :].astype(F32)
-                S.s2[s, path, at, :] = total.astype(BF16)
-                return 0
-
-            lax.fori_loop(0, 4, step, 0)
-        return [
-            push(
-                S.s2.at[s, path, pl.ds(pl.multiple_of(ring_index(1 - path, d) * q2, q2), q2), :],
-                S.r2.at[s, path, d - 1], S.s2s.at[s, path, d - 1], S.s2r.at[s, path, d - 1],
-                ring_target(1 - path, d),
-            )
-            for d in (1, 2, 3) for path in range(2)
-        ]
-
-    near = lax.div(z, 4) == p
-
-    def third_exchange(s, copies):
-        for copy in copies:
-            copy.wait_recv()
-        for path in range(2):
-            mine = pl.ds(pl.multiple_of(ring_index(1 - path, 0) * q2, q2), q2)
-            total = S.s2[s, path, mine, :].astype(F32)
+        mine = pl.ds(pl.multiple_of(second_place * q2, q2), q2)
+        for h in range(2):
+            total = S.s2[s, h, mine, :].astype(F32)
             for d in range(3):
-                total = total + S.r2[s, path, d].astype(F32)
+                total = total + S.r2[s, d, h].astype(F32)
             S.t3[0:q2, :] = total
             for k in range(4):
-                S.s3[s, k, path] = S.t3[BLOCK * k : BLOCK * k + 16, :].astype(BF16)
-        for k in range(4):
-            target_z = 4 * p + k
-            stays = (target_z == z) & (p == s)
-            copy = pltpu.make_async_remote_copy(
-                src_ref=S.s3.at[s, k], dst_ref=S.r3.at[z], send_sem=S.s3s.at[s, k],
-                recv_sem=S.s3r.at[z], device_id=dev(target_z * NX + x, s, y), device_id_type=MESH,
-            )
-
-            @pl.when(jnp.logical_not(stays))
+                S.s3[s, 4 * h + k] = S.t3[BLOCK * k : BLOCK * k + 16, :].astype(BF16)
+        for dz in range(1, NZ):
+            third_copy(s, dz).start()
+
+        @pl.when(p != s)
+        def _():
+            third_copy(s, 0).start()
+
+        @pl.when(p == s)
+        def _():
+            S.r3[0, 0] = S.s3[s, z]
+
+    def third_sum():
+        for s in range(2):
+            for dz in range(1, NZ):
+                third_copy(s, dz).wait_send()
+
+            @pl.when(p != s)
             def _():
-                copy.start()
-
-            @pl.when(stays)
-            def _():
-                S.r3[z] = S.s3[s, k]
-
-    def finish_third():
-        for s in range(2):
-            for k in range(4):
-                target_z = 4 * p + k
-                stays = (target_z == z) & (p == s)
-
-                @pl.when(jnp.logical_not(stays))
-                def _():
+                third_copy(s, 0).wait_send()
+        for rel, at in ((0, own_col), (1, oth_col)):
+            total = jnp.zeros((16, HALF), F32)
+            for dz in range(NZ):
+                if (dz, rel) != (0, 0):
                     pltpu.make_async_remote_copy(
-                        src_ref=S.s3.at[s, k], dst_ref=S.r3.at[z], send_sem=S.s3s.at[s, k],
-                        recv_sem=S.s3r.at[z], device_id=dev(target_z * NX + x, s, y),
-                        device_id_type=MESH,
-                    ).wait_send()
-        for k in range(NZ):
-            @pl.when(jnp.logical_not((z == k) & near))
-            def _():
-                pltpu.make_async_remote_copy(
-                    src_ref=S.s3.at[0, 0], dst_ref=S.r3.at[k], send_sem=S.s3s.at[0, 0],
-                    recv_sem=S.s3r.at[k], device_id=along(0, q), device_id_type=MESH,
-                ).wait_recv()
-        for path in range(2):
-            total = S.r3[0, path].astype(F32)
-            for k in range(1, NZ):
-                total = total + S.r3[k, path].astype(F32)
+                        src_ref=S.s3.at[0, 0], dst_ref=S.r3.at[dz, rel], send_sem=S.s3s.at[0, 0],
+                        recv_sem=S.s3r.at[dz, rel], device_id=along(0, q), device_id_type=MESH,
+                    ).wait_recv()
+                total = total + S.r3[dz, rel].astype(F32)
             for k in range(BLOCK):
-                gw_ref[k, :, path * HALF : (path + 1) * HALF] = total[k : k + 1]
+                gw_ref[k, :, pl.ds(at, HALF)] = total[k : k + 1]
+
+    loc[2].wait()
+    loc[3].wait()
+    cotangent1 = send_cotangent(1)
+    par_copy.wait_recv()
+    copies = send_table(0, *conv_forward(0, halo_copies))
+    lax.fori_loop(0, steps, back_step(0, None), 0)
+    loc[1].wait()
+    w_copy.wait_recv()
+    act_grad(1)
+    mean, scale = moments(0, copies)
+
+    def norm_step(b, _):
+        base = base_of(b)
+        m, v = normalize(0, base, member(base), mean, scale)
+        for c in range(TILES):
+            normed = (S.y[0, c, pl.ds(base + RIM, STEP), :] - m) * v
+            S.nrm[0, c, pl.ds(base, STEP), :] = normed
+            _, pre, sig = activate(0, base, c, normed)
+            S.act[0, pl.ds(base, STEP), cols(c)] = (pre * sig).astype(BF16)
+        return 0
+
+    lax.fori_loop(0, steps, norm_step, 0)
+    S.hx[0] = dot(S.act[0], S.w[0, :, pl.ds(oth_col, HALF)]).astype(BF16)
+    copy = push(S.hx.at[0], S.hx.at[1], S.xs.at[0], S.xr.at[0], along(0, q))
+    S.part[...] = dot(S.act[0], S.w[0, :, pl.ds(own_col, HALF)])
+    turn_activation(0)
+    copy.wait_recv()
+
+    def out_step(b, _):
+        base = base_of(b)
+        at = pl.ds(base, STEP)
+        S.h1[at, :] = (S.hb[at, :].astype(F32) + (S.part[at, :] + S.hx[1, at, :].astype(F32))).astype(BF16)
+        return 0
+
+    lax.fori_loop(0, steps, out_step, 0)
+    halo_copies = send_halo(1, S.h1.at[pl.ds(0, RIM), :], S.h1.at[pl.ds(ROWS - RIM, RIM), :])
+    for c in range(TILES):
+        S.xf[1, c, RIM : RIM + ROWS, :] = S.h1[:, cols(c)].astype(F32)
+
+    copies = send_table(1, *conv_forward(1, halo_copies))
+
+    halo_y = send_edges(4, 2, S.y.at[1])
+    activation0 = push_activation(0)
+    back_inner(1, S.y.at[1])
+    mean, scale = moments(1, copies)
 
     copies = send_table(2, *pre_grad(1, mean, scale))
-    weight_partial(1)
-    halo_copies = conv_grad(1, 2, copies)
-    first1 = first_exchange(1)
-
-    def while_away():
-        kernel_grad(1, 0, 4)
-        take_halo(2, halo_copies, S.cg)
-
-    conv_backward(1, while_away)
+    halo_n = send_edges(2, 1, S.cg)
+    back_inner(2, S.cg)
+    take_halo(4, halo_y, S.y.at[1])
+    back_outer(1, S.y.at[1])
+    take_halo(2, halo_n, S.cg)
+    back_outer(2, S.cg)
+    mean_a, mean_b = take_table(2, copies)
+    pass_down(mean, mean_a, mean_b)
     copy = push(S.gbuf.at[0, p], S.gbuf.at[0, p], S.xs.at[1], S.xr.at[1], along(0, q))
+    cotangent0 = send_cotangent(0)
+    turn_activation(1)
+    activation1 = push_activation(1)
     copy.wait_recv()
 
     act_grad(0)
     copies = send_table(3, *pre_grad(0, None, None))
-    weight_partial(0)
-    kernel_grad(1, 4, steps)
+    conv_grad(1, mean_a, mean_b)
+    kernel_grad(1, 0, steps)
     keep_small(1)
-    second1 = second_exchange(1, first1)
-    halo_copies = conv_grad(0, 3, copies)
-    first0 = first_exchange(0)
+    conv_grad(0, *take_table(3, copies))
+    halo_copies = send_edges(3, 0, S.cg)
     kernel_grad(0, 0, steps)
     keep_small(0)
 
@@ -577,7 +628,8 @@
         )
         for n, (dx, dy) in enumerate(PLANE[1:])
     ]
-    third_exchange(1, second1)
+    second1 = first_sum(1, activation1 + cotangent1)
+    second0 = first_sum(0, activation0 + cotangent0)
     conv_backward(0, lambda: take_halo(3, halo_copies, S.cg))
     for copy in small:
         copy.wait_recv()
@@ -589,7 +641,8 @@
         push(S.zb.at[z], S.zb.at[z], S.zs.at[dz - 1], S.zr.at[dz - 1], depth(dz, p))
         for dz in range(1, NZ)
     ]
-    second0 = second_exchange(0, first0)
+    second_sum(1, second1)
+    second_sum(0, second0)
     for dz in range(1, NZ):
         from_z = lax.rem(z + NZ - dz, NZ)
         pltpu.make_async_remote_copy(
@@ -606,8 +659,7 @@
         push(S.fs.at[core[rel]], S.fin.at[p, place], S.gs.at[n], S.gr.at[n], plane(dx, dy, core[rel]))
         for n, (dx, dy, rel) in enumerate(GATHER)
     ]
-    third_exchange(0, second0)
-    finish_third()
+    third_sum()
     for copy in small:
         copy.wait_recv()
     for h in range(2):

time: 99.3 us -> 92.7 us (0.934)
  Pallas kernels: 98.5 us -> 91.1 us
    pallas_call x1, Pallas kernels: 96.6 us -> 89.2 us  [body(): pl.pallas_call(kern, out_shape=(jax.ShapeDtypeStruct((1, ROWS, HALF), BF1...]
where the time goes in v3:
time: 92.7 us; the launch traced here: 91.8 us
  Pallas kernels  91.1 us (98%)
    pallas_call x1, Pallas kernels, body(): pl.pallas_call(kern, out_shape=(jax.ShapeDtypeStruct((1, ROWS, HALF), BF1...  89.2 us
    pallas_call x1, Pallas kernels, body(): pl.pallas_call(relay_kernel, out_shape=tuple((jax.ShapeDtypeStruct(r.shap...  1.95 us

profile of v3, /device:TPU:1, one launch (start us, length us, event | category | flops | bytes accessed | tf_op | source)
XLA Modules:
  0.0 91.8 jit_solution(599799306803297631)
XLA Ops:
  0.6 89.2 %shard_map.110 = (bf16[1,256,768]{2,1,0:T(8,128)(2,1)}, f32[12,1,1536]{2,1,0:T(1,128)}, f32[1,32,1536]{2,1,0:T(8,128)}, f32[1,1536]{1,0:T(1,128)}, f32[1,1536]{1,0:T(1,128)}) custom-call(bf16[1,256,1536]{2,1,0:T(8,128)(2,1)} %refs_0_.1, bf16[1,256,1536]{2,1,0:T(8,128)(2,1)} %refs_1_.1, s32[1,32]{1,0:T(1,128)} %refs_2_.1, bf16[1,1536,1536]{2,1,0:T(8,128)(2,1)} %refs_3_.1, ...), custom_call_target="tpu_custom_call" | custom-call | tf_op jit(solution)/shard_map/pallas_call | solution.py:691
  89.8 1.9 %shard_map.111 = (bf16[1,256,768]{2,1,0:T(8,128)(2,1)}, f32[12,1,1536]{2,1,0:T(1,128)}, f32[1,32,1536]{2,1,0:T(8,128)}, f32[1,1536]{1,0:T(1,128)}, f32[1,1536]{1,0:T(1,128)}) custom-call(bf16[1,256,768]{2,1,0:T(8,128)(2,1)} %get-tuple-element.15.refs_0_, f32[12,1,1536]{2,1,0:T(1,128)} %get-tuple-element.16.refs_1_, ...), custom_call_target="tpu_custom_call" | custom-call | tf_op jit(solution)/shard_map/pallas_call | solution.py:707

commit v4 on v3

--- a/solution.py
+++ b/solution.py
@@ -18,8 +18,10 @@
 STEP, GROUP = 32, 3
 PADDED = ROWS + 2 * RIM
 
-PLANE = [(dx, dy) for dx in range(NX) for dy in range(NY)]
-OFFSETS = [(s, rel) for s in (-2, -1, 0, 1, 2) for rel in (0, 1) if (s, rel) != (0, 0)]
+RING = (2, 1, 3, 0)
+PLANE = sorted(((dx, dy) for dx in RING for dy in RING), key=lambda at: -min(at[0], 4 - at[0]) - min(at[1], 4 - at[1]))
+OFFSETS = [(s, rel) for s in (2, -2, 1, -1, 0) for rel in (0, 1) if (s, rel) != (0, 0)]
+DEPTH = (4, 3, 5, 2, 6, 1, 7)
 GATHER = [(dx, dy, rel) for dx, dy in PLANE for rel in (0, 1) if (dx, dy, rel) != (0, 0, 0)]
 
 
@@ -70,7 +72,7 @@
         xs=dma((2,)), xr=dma((2,)),
         ts=dma((4, 9)), tr=dma((4, 9)),
         tas=dma((2, 4, 2)), tar=dma((2, 4, 2)),
-        gqs=dma((2, 3)), gqr=dma((2, 3)),
+        gqs=dma((2, 4)), gqr=dma((2, 4)),
         s2s=dma((2, 3)), s2r=dma((2, 3)),
         s3s=dma((2, NZ)), s3r=dma((NZ, 2)),
         as_=dma((15,)), ar_=dma((15,)),
@@ -453,10 +455,20 @@
     def second_ring(d):
         return plane(d * (1 - p), d * p, p)
 
-    def send_cotangent(s):
+    def send_cotangent(s, distances):
         return [
             push(S.gbuf.at[s, p], S.gq.at[s, d - 1], S.gqs.at[s, d - 1], S.gqr.at[s, d - 1], first_ring(d, p))
-            for d in (1, 3, 2)
+            for d in distances
+        ]
+
+    def forward_cotangent(s):
+        half = ROWS // 2
+        return [
+            push(
+                S.gq.at[s, d - 1, pl.ds(at, half), :], S.gq.at[s, 1, pl.ds(at, half), :],
+                S.gqs.at[s, n], S.gqr.at[s, n], first_ring(d, p),
+            )
+            for d, at, n in ((1, 0, 1), (3, half, 3))
         ]
 
     def turn_activation(s):
@@ -518,7 +530,7 @@
             S.t3[0:q2, :] = total
             for k in range(4):
                 S.s3[s, 4 * h + k] = S.t3[BLOCK * k : BLOCK * k + 16, :].astype(BF16)
-        for dz in range(1, NZ):
+        for dz in DEPTH:
             third_copy(s, dz).start()
 
         @pl.when(p != s)
@@ -551,7 +563,7 @@
 
     loc[2].wait()
     loc[3].wait()
-    cotangent1 = send_cotangent(1)
+    cotangent1 = send_cotangent(1, (2,))
     par_copy.wait_recv()
     copies = send_table(0, *conv_forward(0, halo_copies))
     lax.fori_loop(0, steps, back_step(0, None), 0)
@@ -559,6 +571,7 @@
     w_copy.wait_recv()
     act_grad(1)
     mean, scale = moments(0, copies)
+    cotangent1 += send_cotangent(1, (1, 3))
 
     def norm_step(b, _):
         base = base_of(b)
@@ -605,17 +618,21 @@
     mean_a, mean_b = take_table(2, copies)
     pass_down(mean, mean_a, mean_b)
     copy = push(S.gbuf.at[0, p], S.gbuf.at[0, p], S.xs.at[1], S.xr.at[1], along(0, q))
-    cotangent0 = send_cotangent(0)
+    cotangent0 = send_cotangent(0, (1, 3))
     turn_activation(1)
-    activation1 = push_activation(1)
     copy.wait_recv()
 
     act_grad(0)
     copies = send_table(3, *pre_grad(0, None, None))
+    activation1 = push_activation(1)
     conv_grad(1, mean_a, mean_b)
     kernel_grad(1, 0, steps)
     keep_small(1)
-    conv_grad(0, *take_table(3, copies))
+    mean_a, mean_b = take_table(3, copies)
+    for copy in cotangent0:
+        copy.wait_recv()
+    cotangent0 = forward_cotangent(0)
+    conv_grad(0, mean_a, mean_b)
     halo_copies = send_edges(3, 0, S.cg)
     kernel_grad(0, 0, steps)
     keep_small(0)
@@ -626,7 +643,7 @@
             S.sb.at[lax.rem(x + dx, NX) * NY + lax.rem(y + dy, NY)], S.ar.at[n],
             S.as_.at[n], S.ar_.at[n], plane(dx, dy, p),
         )
-        for n, (dx, dy) in enumerate(PLANE[1:])
+        for n, (dx, dy) in enumerate(PLANE[:-1])
     ]
     second1 = first_sum(1, activation1 + cotangent1)
     second0 = first_sum(0, activation0 + cotangent0)
@@ -639,7 +656,7 @@
     S.zb[z] = total
     small = [
         push(S.zb.at[z], S.zb.at[z], S.zs.at[dz - 1], S.zr.at[dz - 1], depth(dz, p))
-        for dz in range(1, NZ)
+        for dz in DEPTH
     ]
     second_sum(1, second1)
     second_sum(0, second0)

time: 92.7 us -> 86.5 us (0.933)
  Pallas kernels: 91.1 us -> 85.7 us
    pallas_call x1, Pallas kernels: 89.2 us -> 83.8 us  [body(): pl.pallas_call(kern, out_shape=(jax.ShapeDtypeStruct((1, ROWS, HALF), BF1...]
where the time goes in v4:
time: 86.5 us; the launch traced here: 86.4 us
  Pallas kernels  85.7 us (99%)
    pallas_call x1, Pallas kernels, body(): pl.pallas_call(kern, out_shape=(jax.ShapeDtypeStruct((1, ROWS, HALF), BF1...  83.8 us
    pallas_call x1, Pallas kernels, body(): pl.pallas_call(relay_kernel, out_shape=tuple((jax.ShapeDtypeStruct(r.shap...  1.95 us

profile of v4, /device:TPU:1, one launch (start us, length us, event | category | flops | bytes accessed | tf_op | source)
XLA Modules:
  0.0 86.4 jit_solution(10341648753317897889)
XLA Ops:
  0.6 83.8 %shard_map.110 = (bf16[1,256,768]{2,1,0:T(8,128)(2,1)}, f32[12,1,1536]{2,1,0:T(1,128)}, f32[1,32,1536]{2,1,0:T(8,128)}, f32[1,1536]{1,0:T(1,128)}, f32[1,1536]{1,0:T(1,128)}) custom-call(bf16[1,256,1536]{2,1,0:T(8,128)(2,1)} %refs_0_.1, bf16[1,256,1536]{2,1,0:T(8,128)(2,1)} %refs_1_.1, s32[1,32]{1,0:T(1,128)} %refs_2_.1, bf16[1,1536,1536]{2,1,0:T(8,128)(2,1)} %refs_3_.1, ...), custom_call_target="tpu_custom_call" | custom-call | tf_op jit(solution)/shard_map/pallas_call | solution.py:708
  84.4 1.9 %shard_map.111 = (bf16[1,256,768]{2,1,0:T(8,128)(2,1)}, f32[12,1,1536]{2,1,0:T(1,128)}, f32[1,32,1536]{2,1,0:T(8,128)}, f32[1,1536]{1,0:T(1,128)}, f32[1,1536]{1,0:T(1,128)}) custom-call(bf16[1,256,768]{2,1,0:T(8,128)(2,1)} %get-tuple-element.15.refs_0_, f32[12,1,1536]{2,1,0:T(1,128)} %get-tuple-element.16.refs_1_, ...), custom_call_target="tpu_custom_call" | custom-call | tf_op jit(solution)/shard_map/pallas_call | solution.py:724

commit v5 on v4

--- a/solution.py
+++ b/solution.py
@@ -629,11 +629,11 @@
     kernel_grad(1, 0, steps)
     keep_small(1)
     mean_a, mean_b = take_table(3, copies)
+    conv_grad(0, mean_a, mean_b)
+    halo_copies = send_edges(3, 0, S.cg)
     for copy in cotangent0:
         copy.wait_recv()
     cotangent0 = forward_cotangent(0)
-    conv_grad(0, mean_a, mean_b)
-    halo_copies = send_edges(3, 0, S.cg)
     kernel_grad(0, 0, steps)
     keep_small(0)
 

time: 86.5 us -> 86.1 us (level)
  no operation moved by 1% of the time
where the time goes in v5:
time: 86.1 us; the launch traced here: 86 us
  Pallas kernels  85.4 us (99%)
    pallas_call x1, Pallas kernels, body(): pl.pallas_call(kern, out_shape=(jax.ShapeDtypeStruct((1, ROWS, HALF), BF1...  83.4 us
    pallas_call x1, Pallas kernels, body(): pl.pallas_call(relay_kernel, out_shape=tuple((jax.ShapeDtypeStruct(r.shap...  1.95 us

profile of v5, /device:TPU:1, one launch (start us, length us, event | category | flops | bytes accessed | tf_op | source)
XLA Modules:
  0.0 86.0 jit_solution(10416473275354366405)
XLA Ops:
  0.6 83.4 %shard_map.110 = (bf16[1,256,768]{2,1,0:T(8,128)(2,1)}, f32[12,1,1536]{2,1,0:T(1,128)}, f32[1,32,1536]{2,1,0:T(8,128)}, f32[1,1536]{1,0:T(1,128)}, f32[1,1536]{1,0:T(1,128)}) custom-call(bf16[1,256,1536]{2,1,0:T(8,128)(2,1)} %refs_0_.1, bf16[1,256,1536]{2,1,0:T(8,128)(2,1)} %refs_1_.1, s32[1,32]{1,0:T(1,128)} %refs_2_.1, bf16[1,1536,1536]{2,1,0:T(8,128)(2,1)} %refs_3_.1, ...), custom_call_target="tpu_custom_call" | custom-call | tf_op jit(solution)/shard_map/pallas_call | solution.py:708
  84.0 1.9 %shard_map.111 = (bf16[1,256,768]{2,1,0:T(8,128)(2,1)}, f32[12,1,1536]{2,1,0:T(1,128)}, f32[1,32,1536]{2,1,0:T(8,128)}, f32[1,1536]{1,0:T(1,128)}, f32[1,1536]{1,0:T(1,128)}) custom-call(bf16[1,256,768]{2,1,0:T(8,128)(2,1)} %get-tuple-element.15.refs_0_, f32[12,1,1536]{2,1,0:T(1,128)} %get-tuple-element.16.refs_1_, ...), custom_call_target="tpu_custom_call" | custom-call | tf_op jit(solution)/shard_map/pallas_call | solution.py:724
